TPU v7x, 512 devices: a whole 4x8x8 slice. The times are simulated.
512 devices in a mesh: dp: 32 (over z, x), chan: 16 (over y, core).
Axes of the slice: x: 4, y: 8, z: 8, core: 2. Of those that a mesh axis runs over, the one named last changes fastest.
Arguments:
- tokens: bfloat16 [4096, 2560], P('dp', 'chan'), may hold values from -6 to 6
- norm_gain: float32 [2560], replicated, may hold values from 0.5 to 1.5
- in_weight: bfloat16 [2560, 2, 5120], P(None, None, 'chan'), may hold values from -0.125 to 0.125
- conv_weight: float32 [4, 5120], P(None, 'chan'), may hold values from -3 to 3
- conv_bias: float32 [5120], P('chan'), may hold values from -3 to 3
- proj_weight: bfloat16 [5120, 192], P('chan'), may hold values from -0.078125 to 0.078125
- dt_weight: bfloat16 [160, 5120], P(None, 'chan'), may hold values from -0.5 to 0.5
- dt_bias: float32 [5120], P('chan'), may hold values from -6 to -2
- decay_rate: float32 [5120, 16], P('chan'), may hold values from 1e-05 to 8
- skip_gain: float32 [5120], P('chan'), may hold values from 0.5 to 1.5
- doc_starts: int32 [4096], P('dp'), may hold values from 0 to 1, as said below
- group_target: int32 [512], P('dp'), may hold values from 0 to 511, as said below
Outputs:
- mixed: bfloat16 [4096, 5120], P('dp', 'chan')
Inputs may be any that keep to these rules, and one draw needn't show every extreme that they name: doc_starts is 1 at the first byte of each document; its entry 0 is 1. group_target is a permutation of the group positions; every device receives 16 groups; every device sends its 16 groups to 16 distinct devices, exactly 1 group to each of them.
All inputs are finite; a program needn't handle non-finite values.
Results may differ from a plain program's by a relative error of at most 0.014.
Values may be sent and summed in bfloat16 or wider, within the bound.
No kernel may reach another device: no remote copies, remote signals or barrier semaphores. Data moves between devices by JAX's collectives and lax.ppermute only.
A program may use at most 64 MiB of HBM per device.

v0:
```python
import functools
import math

import jax
import jax.numpy as jnp
from jax import lax
from jax.experimental import pallas as pl
from jax.experimental.pallas import tpu as pltpu
from jax.sharding import PartitionSpec as P

EPSILON = 1e-05
LOG2E = math.log2(math.e)
FAR = 1e30
F32 = jnp.float32
BF16 = jnp.bfloat16

VMEM = pl.BlockSpec(memory_space=pltpu.VMEM)
SMEM = pl.BlockSpec(memory_space=pltpu.SMEM)

NN = (((1,), (0,)), ((), ()))
NT = (((1,), (1,)), ((), ()))
TN = (((0,), (0,)), ((), ()))


def dot(a, b, dims=NN):
    return lax.dot_general(a, b, dims, preferred_element_type=F32)


def iota(shape, dim):
    return lax.broadcasted_iota(jnp.int32, shape, dim)


def call(body, outs, specs, args, scratch=(), limit=24):
    return pl.pallas_call(
        body,
        out_shape=outs,
        in_specs=specs,
        out_specs=jax.tree.map(lambda _: VMEM, outs),
        scratch_shapes=list(scratch),
        compiler_params=pltpu.CompilerParams(vmem_limit_bytes=limit << 20),
    )(*args)


def pack_body(slots, target, me, tok_ref, starts_ref, out_ref):
    features, tokens = tok_ref.shape
    rows = out_ref.shape[0]
    lane = iota((1, tokens), 1)
    where_to = jnp.zeros((1, tokens), jnp.int32)
    for group in range(slots):
        where_to = jnp.where((lane >> 3) == group, target[group], where_to)
    dev = where_to // slots
    slot = where_to % slots
    inner = lane & 7
    main_key = dev * 16 + inner
    tail_key = jnp.where((slot == slots - 1) & (inner >= 5), (dev + 1) * 16 + inner + 3, -1)
    slot_key = jnp.where(inner == 0, dev * 16 + 11, -1)
    row = iota((rows, tokens), 0)
    pick = jnp.where((row == main_key) | (row == tail_key), 1.0, 0.0)
    mark = jnp.where(row == slot_key, (slot + 1).astype(F32), 0.0)
    both = jnp.concatenate([pick, mark], axis=1).astype(BF16)
    values = jnp.concatenate([tok_ref[...], jnp.ones((features, tokens), BF16)], axis=1)
    pieces = dot(both, values, NT)
    fresh = 1.0 - jnp.broadcast_to(starts_ref[...].astype(F32), (8, tokens))
    lane8 = iota((8, tokens), 1)
    next_one = pltpu.roll(fresh, tokens - 1, 1)
    next_two = pltpu.roll(fresh, tokens - 2, 1)
    open_tail = jnp.where(
        lane8 == tokens - 1, 1.0, jnp.where(lane8 == tokens - 2, next_one, next_one * next_two)
    )
    open_tail = jnp.where(lane8 >= tokens - 3, open_tail, 0.0)[:1]
    open_wide = jnp.concatenate([open_tail, jnp.zeros((1, features - tokens), F32)], axis=1)
    row_wide = iota((rows, features), 0)
    pieces = jnp.where(row_wide == (me[0] + 1) * 16 + 12, open_wide, pieces)
    out_ref[...] = pieces.astype(BF16)


def place_body(in_ref, gain_ref, out_ref):
    rows, features = in_ref.shape
    tokens = out_ref.shape[1]
    arrived = in_ref[...]
    head = arrived[:, :tokens].astype(F32).reshape(rows // 16, 16, tokens)
    label = jnp.broadcast_to(head[:, 11:12, :], head.shape).reshape(rows, tokens)
    open_tail = jnp.sum(head, axis=0)[12:13]
    row = (iota((rows, tokens), 0) & 15).astype(F32)
    lane = iota((rows, tokens), 1)
    want = (((lane >> 3) + 1) * 16 + (lane & 7)).astype(F32)
    main = jnp.where(label * 16.0 + row == want, 1.0, 0.0)
    tail_row = jnp.where(lane >= tokens - 3, lane - (tokens - 3) + 8, -1).astype(F32)
    tail = jnp.where(row == tail_row, 1.0, 0.0)
    pick = jnp.concatenate([main, tail], axis=1).astype(BF16)
    found = dot(arrived, pick, TN)
    gain = gain_ref[...]
    x_main = found[:, :tokens]
    x_tail = found[:, tokens:] * open_tail
    main_sq = jnp.sum(x_main * x_main, axis=0, keepdims=True)
    tail_sq = jnp.sum(x_tail * x_tail, axis=0, keepdims=True)
    out_ref[0:features, :] = (x_main * gain).astype(BF16)
    x_tail = x_tail * gain
    packed = jnp.zeros((16, tokens), F32)
    for part in range(features // 16):
        shift = (8 * part - (tokens - 8)) % tokens
        packed = packed + pltpu.roll(x_tail[16 * part : 16 * part + 16], shift, 1)
    out_ref[features : features + 16, :] = packed.astype(BF16)
    main_high = main_sq.astype(BF16).astype(F32)
    tail_high = tail_sq.astype(BF16).astype(F32)
    line = iota((16, tokens), 0)
    sums = jnp.where(
        line == 0,
        main_high,
        jnp.where(
            line == 1,
            main_sq - main_high,
            jnp.where(line == 2, tail_high, jnp.where(line == 3, tail_sq - tail_high, 0.0)),
        ),
    )
    out_ref[features + 16 : features + 32, :] = sums.astype(BF16)


def project_body(
    features, in_ref, weight_ref, taps_ref, bias_ref, proj_ref, starts_ref,
    low_ref, act_ref, gate_ref, wide,
):
    count = in_ref.shape[0]
    tokens = in_ref.shape[2]
    channels = act_ref.shape[0]
    taps = taps_ref.shape[1]
    width = count * features
    sums = jnp.zeros((16, tokens), F32)
    for peer in range(count):
        base = peer * features
        wide[base : base + features, 0:tokens] = in_ref[peer, 0:features, :]
        packed = in_ref[peer, features : features + 16, :].astype(F32)
        sums = sums + in_ref[peer, features + 16 : features + 32, :].astype(F32)
        for part in range(features // 16):
            shift = (tokens - 8 - 8 * part) % tokens
            moved = packed if shift == 0 else pltpu.roll(packed, shift, 1)
            wide[base + 16 * part : base + 16 * part + 16, tokens:] = moved.astype(BF16)
    scale_main = lax.rsqrt((sums[0:1] + sums[1:2]) / width + EPSILON)
    scale_tail = lax.rsqrt((sums[2:3] + sums[3:4]) / width + EPSILON)
    both = dot(weight_ref[0:channels, :], wide[...])
    gate = dot(weight_ref[channels:, :], wide[:, 0:tokens])
    x_in = (both[:, :tokens] * scale_main).astype(BF16).astype(F32)
    tail = (both[:, tokens:] * scale_tail).astype(BF16).astype(F32)
    gate = (gate * scale_main).astype(BF16).astype(F32)
    gate_ref[...] = gate * (1.0 / (1.0 + jnp.exp(-gate)))
    fresh = 1.0 - jnp.broadcast_to(starts_ref[...].astype(F32), (8, tokens))
    lane8 = iota((8, tokens), 1)
    lane = iota((channels, tokens), 1)
    convolved = bias_ref[...] + taps_ref[:, taps - 1 : taps] * x_in
    mask = fresh
    for back in range(1, taps):
        if back > 1:
            mask = mask * jnp.where(lane8 < back - 1, 1.0, pltpu.roll(fresh, back - 1, 1))
        behind = pltpu.roll(jnp.where(lane >= tokens - back, tail, x_in), back, 1)
        tap = taps_ref[:, taps - 1 - back : taps - back]
        convolved = convolved + jnp.where(mask[:1] > 0.5, tap * behind, 0.0)
    act = (convolved * (1.0 / (1.0 + jnp.exp(-convolved)))).astype(BF16)
    act_ref[...] = act
    low_ref[...] = dot(proj_ref[...], act).astype(BF16)


def scan_body(
    rank, in_ref, act_ref, dtw_ref, bias_ref, rate_ref, skip_ref, starts_ref,
    out_ref, elapsed_ref, map_ref, send_ref, decay_step, drive_step, hidden,
):
    tokens = in_ref.shape[2]
    states, channels = rate_ref.shape
    low = in_ref[0].astype(F32)
    for peer in range(1, in_ref.shape[0]):
        low = low + in_ref[peer].astype(F32)
    dt_low = low[:rank].astype(BF16)
    in_map = low[rank : rank + states]
    out_map = low[rank + states :]
    raw = dot(dt_low, dtw_ref[...], TN) + bias_ref[...]
    step = jnp.maximum(raw, 0.0) + jnp.log1p(jnp.exp(-jnp.abs(raw)))
    act = jnp.transpose(act_ref[...].astype(F32))
    out_ref[...] = skip_ref[...] * act
    drive_step[...] = step * act
    first = jnp.transpose(jnp.broadcast_to(starts_ref[...].astype(F32), (tokens, tokens)))
    first = first[:, :1]
    step = jnp.where(first > 0.5, FAR, step)
    decay_step[...] = step
    high = step.astype(BF16)
    rest = (step - high.astype(F32)).astype(BF16)
    lower = jnp.where(iota((tokens, tokens), 0) >= iota((tokens, tokens), 1), 1.0, 0.0).astype(BF16)
    elapsed = dot(lower, high) + dot(lower, rest)
    elapsed_ref[...] = elapsed
    spread = jnp.where((iota((states, tokens), 1) & (states - 1)) == iota((states, tokens), 0), 1.0, 0.0)
    maps = dot(out_map.astype(BF16), spread.astype(BF16), TN)
    own = (iota((tokens, tokens), 1) // states) == (iota((tokens, tokens), 0) & 7)
    maps = jnp.where(own, maps, 0.0).astype(BF16)
    map_ref[...] = maps
    rate = rate_ref[...] * (-LOG2E)
    state = jnp.zeros((states, channels), F32)
    for block in range(tokens // 8):
        for inner in range(8):
            t = block * 8 + inner
            decay = jnp.exp2(decay_step[t : t + 1, :] * rate)
            state = decay * state + drive_step[t : t + 1, :] * in_map[:, t : t + 1]
            hidden[inner * states : (inner + 1) * states, :] = state.astype(BF16)
        out_ref[block * 8 : block * 8 + 8, :] += dot(maps[block * 8 : block * 8 + 8], hidden[...])
    last = elapsed[tokens - 1 : tokens]
    last_high = last.astype(BF16).astype(F32)
    line = iota((16, channels), 0)
    ends = jnp.where(line == 0, last_high, jnp.where(line == 1, last - last_high, 0.0)).astype(BF16)
    final = state.astype(BF16)
    for peer in range(send_ref.shape[0]):
        send_ref[peer, 0:states, :] = final
        send_ref[peer, states : states + 16, :] = ends


def finish_body(me, in_ref, rate_ref, out_in_ref, elapsed_ref, map_ref, gate_ref, mixed_ref, carried):
    states, channels = rate_ref.shape
    tokens = elapsed_ref.shape[0]
    rate = rate_ref[...] * (-LOG2E)
    state = jnp.zeros((states, channels), F32)
    for peer in range(in_ref.shape[0]):
        ends = in_ref[peer, states : states + 16, :].astype(F32)
        length = ends[0:1] + ends[1:2]
        final = in_ref[peer, 0:states, :].astype(F32)
        state = jnp.where(peer < me[0], jnp.exp2(length * rate) * state + final, state)
    corrected = []
    for block in range(tokens // 8):
        for inner in range(8):
            t = block * 8 + inner
            value = jnp.exp2(elapsed_ref[t : t + 1, :] * rate) * state
            carried[inner * states : (inner + 1) * states, :] = value.astype(BF16)
        corrected.append(
            out_in_ref[block * 8 : block * 8 + 8, :]
            + dot(map_ref[block * 8 : block * 8 + 8, :], carried[...])
        )
    scanned = jnp.transpose(jnp.concatenate(corrected, axis=0))
    mixed_ref[...] = (scanned * gate_ref[...]).astype(BF16)


def local(
    tokens, norm_gain, in_weight, conv_weight, conv_bias, proj_weight, dt_weight, dt_bias,
    decay_rate, skip_gain, doc_starts, group_target,
):
    peers = lax.axis_size("dp")
    row_count, features = tokens.shape
    slots = group_target.shape[0]
    width = in_weight.shape[0]
    channels = in_weight.shape[2]
    rank = dt_weight.shape[0]
    states = decay_rate.shape[1]
    shape = jax.ShapeDtypeStruct
    me = lax.axis_index("dp").astype(jnp.int32).reshape(1)
    starts = doc_starts.reshape(1, row_count)
    my_gain = lax.dynamic_slice_in_dim(norm_gain, lax.axis_index("chan") * features, features)
    my_gain = jnp.broadcast_to(my_gain[:, None], (features, row_count))
    weight = jnp.transpose(in_weight, (1, 2, 0)).reshape(2 * channels, width)
    rate = decay_rate.T

    pieces = call(
        functools.partial(pack_body, slots),
        shape((peers * 16, features), BF16),
        [SMEM, SMEM, VMEM, VMEM],
        (group_target, me, tokens.T, starts),
    )
    arrived = lax.all_to_all(pieces.reshape(peers, 16, features), "dp", 0, 0, tiled=True)
    payload = call(
        place_body,
        shape((features + 32, row_count), BF16),
        [VMEM, VMEM],
        (arrived.reshape(peers * 16, features), my_gain),
    )
    gathered = lax.all_gather(payload, "chan", axis=0)
    low, act, gate = call(
        functools.partial(project_body, features),
        (
            shape((rank + 2 * states, row_count), BF16),
            shape((channels, row_count), BF16),
            shape((channels, row_count), F32),
        ),
        [VMEM] * 6,
        (gathered, weight, conv_weight.T, conv_bias[:, None], proj_weight.T, starts),
        [pltpu.VMEM((width, 2 * row_count), BF16)],
    )
    lows = lax.all_gather(low, "chan", axis=0)
    out, elapsed, maps, send = call(
        functools.partial(scan_body, rank),
        (
            shape((row_count, channels), F32),
            shape((row_count, channels), F32),
            shape((row_count, row_count), BF16),
            shape((peers, states + 16, channels), BF16),
        ),
        [VMEM] * 7,
        (lows, act, dt_weight, dt_bias[None, :], rate, skip_gain[None, :], starts),
        [
            pltpu.VMEM((row_count, channels), F32),
            pltpu.VMEM((row_count, channels), F32),
            pltpu.VMEM((8 * states, channels), BF16),
        ],
    )
    ends = lax.all_to_all(send, "dp", 0, 0, tiled=True)
    mixed = call(
        finish_body,
        shape((channels, row_count), BF16),
        [SMEM] + [VMEM] * 6,
        (me, ends, rate, out, elapsed, maps, gate),
        [pltpu.VMEM((8 * states, channels), BF16)],
    )
    return mixed.T


def solution(mesh):
    return jax.shard_map(
        local,
        mesh=mesh,
        in_specs=(
            P("dp", "chan"),
            P(),
            P(None, None, "chan"),
            P(None, "chan"),
            P("chan"),
            P("chan", None),
            P(None, "chan"),
            P("chan"),
            P("chan", None),
            P("chan"),
            P("dp"),
            P("dp"),
        ),
        out_specs=P("dp", "chan"),
        check_vma=False,
    )
```

profile of v0, /device:TPU:1, one launch (start us, length us, event | category | flops | bytes accessed | tf_op | source)
XLA Modules:
  0.0 101.3 jit_solution(3081753490199899095)
XLA Ops:
  0.0 0.8 copy-done.4
  0.8 0.7 copy-done.5
  1.4 0.7 copy-done.7
  2.1 1.5 %shard_map.118 = bf16[512,160]{1,0:T(8,128)(2,1)} custom-call(s32[16]{0:T(128)S(1)} %copy-done.7, s32[1]{0:T(128)} %bitcast.me, bf16[160,128]{1,0:T(8,128)(2,1)S(1)} %bitcast.22, s32[1,128]{1,0:T(1,128)S(1)} %bitcast.23), custom_call_target="tpu_custom_call" | custom-call | tf_op jit(solution)/shard_map/pallas_call | solution.py:34
  3.6 13.7 %all-to-all-start = ((bf16[32,16,160]{2,1,0:T(8,128)(2,1)}), bf16[32,16,160]{2,1,0:T(8,128)(2,1)S(1)}, u32[]{:S(2)}, u32[]{:S(2)}) async-start(bf16[32,16,160]{2,1,0:T(8,128)(2,1)} %bitcast.3), calls=%async_computation | async-start | bytes 524288 | tf_op jit(solution)/shard_map/all_to_all | solution.py:261
  17.3 0.7 broadcast_in_dim.17.bias_ref
  18.0 0.7 broadcast_in_dim.18.skip_ref
  18.7 0.8 copy.14
  19.5 0.8 broadcast_in_dim.19.bias_ref
  20.3 0.8 dynamic_slice.3
  21.1 7.4 %all-to-all-done = bf16[32,16,160]{2,1,0:T(8,128)(2,1)S(1)} async-done(((bf16[32,16,160]{2,1,0:T(8,128)(2,1)}), bf16[32,16,160]{2,1,0:T(8,128)(2,1)S(1)}, u32[]{:S(2)}, u32[]{:S(2)}) %all-to-all-start) | async-done | bytes 163872 | tf_op jit(solution)/shard_map/all_to_all | solution.py:261
  28.5 0.1 broadcast_in_dim.15.gain_ref
  28.6 0.0 copy-start.2
  28.6 0.0 copy-start.3
  28.6 0.3 shard_map.119
  28.9 22.0 %all-gather = bf16[3072,128]{1,0:T(8,128)(2,1)S(1)} all-gather(bf16[192,128]{1,0:T(8,128)(2,1)S(1)} %shard_map.119), channel_id=2, replica_groups=mesh['dp'=32,'chan'=16] {'chan'}, dimensions={0}, use_global_device_ids=true | all-gather | bytes 835584 | tf_op jit(solution)/shard_map/all_gather | solution.py:268
  51.0 1.9 %copy-done = bf16[2560,2,320]{0,2,1:T(8,128)(2,1)S(1)} copy-done((bf16[2560,2,320]{0,2,1:T(8,128)(2,1)S(1)}, bf16[2560,2,320]{0,2,1:T(8,128)(2,1)}, u32[]{:S(2)}) %copy-start) | copy-done | bytes 3276824
  52.9 0.9 copy-done.1
  53.8 0.7 copy-done.6
  54.5 1.4 %shard_map.120 = (bf16[192,128]{1,0:T(8,128)(2,1)S(1)}, bf16[320,128]{1,0:T(8,128)(2,1)S(1)}, f32[320,128]{1,0:T(8,128)S(1)}) custom-call(bf16[16,192,128]{2,1,0:T(8,128)(2,1)S(1)} %bitcast.15, bf16[640,2560]{1,0:T(8,128)(2,1)S(1)} %bitcast.14, f32[320,4]{1,0:T(8,128)S(1)} %bitcast.18, f32[320,1]{1,0:T(8,128)S(1)} %broadcast_in_dim.19.bias_ref, ...), custom_call_target="tpu_custom_call" | custom-call | tf_op jit(solution)/shard_map/pallas_call | solution.py:34
  55.9 17.1 %all-gather.1 = bf16[3072,128]{1,0:T(8,128)(2,1)S(1)} all-gather(bf16[192,128]{1,0:T(8,128)(2,1)S(1)} %get-tuple-element.12), channel_id=3, replica_groups=mesh['dp'=32,'chan'=16] {'chan'}, dimensions={0}, use_global_device_ids=true | all-gather | bytes 835584 | tf_op jit(solution)/shard_map/all_gather | solution.py:280
  73.0 1.4 %shard_map.121 = (f32[128,320]{1,0:T(8,128)S(1)}, f32[128,320]{1,0:T(8,128)S(1)}, bf16[128,128]{1,0:T(8,128)(2,1)S(1)}, bf16[32,32,320]{2,1,0:T(8,128)(2,1)S(1)}) custom-call(bf16[16,192,128]{2,1,0:T(8,128)(2,1)S(1)} %bitcast.16, bf16[320,128]{1,0:T(8,128)(2,1)S(1)} %get-tuple-element.13.act_ref, bf16[160,320]{1,0:T(8,128)(2,1)S(1)} %copy-done.2, ...), custom_call_target="tpu_custom_call" | custom-call | tf_op jit(solution)/shard_map/pallas_call | solution.py:34
  74.4 25.2 %all_to_all.10.in_ref = bf16[32,32,320]{2,1,0:T(8,128)(2,1)S(1)} all-to-all(bf16[32,32,320]{2,1,0:T(8,128)(2,1)S(1)} %get-tuple-element.14), channel_id=1, replica_groups=mesh['dp'=32,'chan'=16] {'dp'}, dimensions={0} | all-to-all | bytes 1310720 | tf_op jit(solution)/shard_map/all_to_all | solution.py:297
  99.7 1.6 %shard_map.122 = bf16[320,128]{1,0:T(8,128)(2,1)} custom-call(s32[1]{0:T(128)} %bitcast.me, bf16[32,32,320]{2,1,0:T(8,128)(2,1)S(1)} %all_to_all.10.in_ref, f32[16,320]{1,0:T(8,128)S(1)} %bitcast.21, f32[128,320]{1,0:T(8,128)S(1)} %get-tuple-element.15.out_in_ref, f32[128,320]{1,0:T(8,128)S(1)} %get-tuple-element.16.elapsed_ref, ...), custom_call_target="tpu_custom_call" | custom-call | tf_op jit(solution)/shard_map/pallas_call | solution.py:34
  (8 shorter events, 0.0 us)
Async XLA Ops:
  0.0 0.8 copy-start.4
  0.8 0.7 copy-start.5
  1.4 0.7 copy-start.7
  3.6 24.9 %all-to-all-start = ((bf16[32,16,160]{2,1,0:T(8,128)(2,1)}), bf16[32,16,160]{2,1,0:T(8,128)(2,1)S(1)}, u32[]{:S(2)}, u32[]{:S(2)}) async-start(bf16[32,16,160]{2,1,0:T(8,128)(2,1)} %bitcast.3), calls=%async_computation | async-start | bytes 524288 | tf_op jit(solution)/shard_map/all_to_all | solution.py:261
  28.6 44.4 %copy-start.2 = (bf16[160,320]{1,0:T(8,128)(2,1)S(1)}, bf16[160,320]{1,0:T(8,128)(2,1)}, u32[]{:S(2)}) copy-start(bf16[160,320]{1,0:T(8,128)(2,1)} %dtw_ref.1) | copy-start | bytes 307204
  28.6 44.4 %copy-start.3 = (f32[320,16]{0,1:T(8,128)S(1)}, f32[320,16]{0,1:T(8,128)}, u32[]{:S(2)}) copy-start(f32[320,16]{0,1:T(8,128)} %param.20) | copy-start | bytes 61444
  51.0 1.9 %copy-start = (bf16[2560,2,320]{0,2,1:T(8,128)(2,1)S(1)}, bf16[2560,2,320]{0,2,1:T(8,128)(2,1)}, u32[]{:S(2)}) copy-start(bf16[2560,2,320]{0,2,1:T(8,128)(2,1)} %param.14) | copy-start | bytes 9830404
  52.9 0.9 copy-start.1
  53.8 0.7 copy-start.6
where the time goes:
time: 102 us; the launch traced here: 101 us
  blocking collectives  64.3 us (63%)
  starting transfers between devices  13.7 us (13%)
  local copies, waits for them, and re-layouts  9.42 us (9%)
  waiting for transfers between devices  7.41 us (7%)
  Pallas kernels  6.3 us (6%)
    all_to_all x1, blocking collectives, local(): ends = lax.all_to_all(send, 'dp', 0, 0, tiled=True)  25.2 us
    all_gather x1, blocking collectives, local(): gathered = lax.all_gather(payload, 'chan', axis=0)  22 us
    all_gather x1, blocking collectives, local(): lows = lax.all_gather(low, 'chan', axis=0)  17.1 us
    all_to_all x1, starting transfers between devices, local(): lax.all_to_all(pieces.reshape(peers, 16, features), 'dp', 0, 0, tiled=True)  13.7 us
    all_to_all x1, waiting for transfers between devices, local(): lax.all_to_all(pieces.reshape(peers, 16, features), 'dp', 0, 0, tiled=True)  7.41 us
    unnamed x17, local copies, waits for them, and re-layouts  6.41 us
    pallas_call x5, Pallas kernels, call(): pl.pallas_call(body, out_shape=outs, in_specs=specs, out_specs=jax.tree.m...  6.3 us
  transfers between devices with their start and end apart: 1, of which 1 were waited for; matrix products, arithmetic and copies ran while one was open for 4% of the time, Pallas kernels for 0%

commit v1 on v0

--- a/solution.py
+++ b/solution.py
@@ -16,6 +16,7 @@
 
 VMEM = pl.BlockSpec(memory_space=pltpu.VMEM)
 SMEM = pl.BlockSpec(memory_space=pltpu.SMEM)
+HBM = pl.BlockSpec(memory_space=pltpu.HBM)
 
 NN = (((1,), (0,)), ((), ()))
 NT = (((1,), (1,)), ((), ()))
@@ -24,6 +25,10 @@
 
 def dot(a, b, dims=NN):
     return lax.dot_general(a, b, dims, preferred_element_type=F32)
+
+
+def in_hbm(value):
+    return pltpu.with_memory_space_constraint(value, pltpu.HBM)
 
 
 def iota(shape, dim):
@@ -41,7 +46,16 @@
     )(*args)
 
 
-def pack_body(slots, target, me, tok_ref, starts_ref, out_ref):
+def pack_body(slots, me, target_hbm, tok_hbm, starts_hbm, out_ref, starts_ref, target, tok_ref, sems):
+    copies = [
+        pltpu.make_async_copy(target_hbm, target, sems.at[0]),
+        pltpu.make_async_copy(tok_hbm, tok_ref, sems.at[1]),
+        pltpu.make_async_copy(starts_hbm, starts_ref, sems.at[2]),
+    ]
+    for copy in copies:
+        copy.start()
+    for copy in copies:
+        copy.wait()
     features, tokens = tok_ref.shape
     rows = out_ref.shape[0]
     lane = iota((1, tokens), 1)
@@ -72,6 +86,39 @@
     row_wide = iota((rows, features), 0)
     pieces = jnp.where(row_wide == (me[0] + 1) * 16 + 12, open_wide, pieces)
     out_ref[...] = pieces.astype(BF16)
+
+
+def fetch_body(
+    weight_hbm, proj_hbm, dtw_hbm, rate_hbm, taps_hbm, conv_bias_hbm, dt_bias_hbm, skip_hbm,
+    weight_ref, proj_ref, dtw_ref, rate_ref, cols_ref, rows_ref,
+    taps_in, conv_bias, dt_bias, skip, sems,
+):
+    taps, channels = taps_in.shape
+    pairs = (
+        (taps_hbm, taps_in),
+        (conv_bias_hbm, conv_bias),
+        (dt_bias_hbm, dt_bias),
+        (skip_hbm, skip),
+        (weight_hbm.at[0:channels], weight_ref),
+        (proj_hbm, proj_ref),
+        (dtw_hbm, dtw_ref),
+        (rate_hbm, rate_ref),
+    )
+    copies = [
+        pltpu.make_async_copy(source, target, sems.at[index])
+        for index, (source, target) in enumerate(pairs)
+    ]
+    for copy in copies:
+        copy.start()
+    for copy in copies[:4]:
+        copy.wait()
+    bias = conv_bias[...].reshape(1, channels)
+    blank = jnp.zeros((8 - taps - 1, channels), F32)
+    cols_ref[...] = jnp.transpose(jnp.concatenate([taps_in[...], bias, blank], axis=0))
+    rows_ref[0:1, :] = dt_bias[...].reshape(1, channels)
+    rows_ref[1:2, :] = skip[...].reshape(1, channels)
+    for copy in copies[4:]:
+        copy.wait()
 
 
 def place_body(in_ref, gain_ref, out_ref):
@@ -117,13 +164,14 @@
 
 
 def project_body(
-    features, in_ref, weight_ref, taps_ref, bias_ref, proj_ref, starts_ref,
-    low_ref, act_ref, gate_ref, wide,
+    features, taps, in_ref, weight_ref, weight_hbm, taps_ref, proj_ref, starts_ref,
+    low_ref, act_ref, gate_ref, wide, gate_weight, sem,
 ):
     count = in_ref.shape[0]
     tokens = in_ref.shape[2]
     channels = act_ref.shape[0]
-    taps = taps_ref.shape[1]
+    fetch = pltpu.make_async_copy(weight_hbm.at[channels:], gate_weight, sem)
+    fetch.start()
     width = count * features
     sums = jnp.zeros((16, tokens), F32)
     for peer in range(count):
@@ -137,16 +185,13 @@
             wide[base + 16 * part : base + 16 * part + 16, tokens:] = moved.astype(BF16)
     scale_main = lax.rsqrt((sums[0:1] + sums[1:2]) / width + EPSILON)
     scale_tail = lax.rsqrt((sums[2:3] + sums[3:4]) / width + EPSILON)
-    both = dot(weight_ref[0:channels, :], wide[...])
-    gate = dot(weight_ref[channels:, :], wide[:, 0:tokens])
+    both = dot(weight_ref[...], wide[...])
     x_in = (both[:, :tokens] * scale_main).astype(BF16).astype(F32)
     tail = (both[:, tokens:] * scale_tail).astype(BF16).astype(F32)
-    gate = (gate * scale_main).astype(BF16).astype(F32)
-    gate_ref[...] = gate * (1.0 / (1.0 + jnp.exp(-gate)))
     fresh = 1.0 - jnp.broadcast_to(starts_ref[...].astype(F32), (8, tokens))
     lane8 = iota((8, tokens), 1)
     lane = iota((channels, tokens), 1)
-    convolved = bias_ref[...] + taps_ref[:, taps - 1 : taps] * x_in
+    convolved = taps_ref[:, taps : taps + 1] + taps_ref[:, taps - 1 : taps] * x_in
     mask = fresh
     for back in range(1, taps):
         if back > 1:
@@ -157,10 +202,14 @@
     act = (convolved * (1.0 / (1.0 + jnp.exp(-convolved)))).astype(BF16)
     act_ref[...] = act
     low_ref[...] = dot(proj_ref[...], act).astype(BF16)
+    fetch.wait()
+    gate = dot(gate_weight[...], wide[:, 0:tokens])
+    gate = (gate * scale_main).astype(BF16).astype(F32)
+    gate_ref[...] = gate * (1.0 / (1.0 + jnp.exp(-gate)))
 
 
 def scan_body(
-    rank, in_ref, act_ref, dtw_ref, bias_ref, rate_ref, skip_ref, starts_ref,
+    rank, in_ref, act_ref, dtw_ref, rate_ref, rows_ref, starts_ref,
     out_ref, elapsed_ref, map_ref, send_ref, decay_step, drive_step, hidden,
 ):
     tokens = in_ref.shape[2]
@@ -171,10 +220,10 @@
     dt_low = low[:rank].astype(BF16)
     in_map = low[rank : rank + states]
     out_map = low[rank + states :]
-    raw = dot(dt_low, dtw_ref[...], TN) + bias_ref[...]
+    raw = dot(dt_low, dtw_ref[...], TN) + rows_ref[0:1, :]
     step = jnp.maximum(raw, 0.0) + jnp.log1p(jnp.exp(-jnp.abs(raw)))
     act = jnp.transpose(act_ref[...].astype(F32))
-    out_ref[...] = skip_ref[...] * act
+    out_ref[...] = rows_ref[1:2, :] * act
     drive_step[...] = step * act
     first = jnp.transpose(jnp.broadcast_to(starts_ref[...].astype(F32), (tokens, tokens)))
     first = first[:, :1]
@@ -200,13 +249,19 @@
             hidden[inner * states : (inner + 1) * states, :] = state.astype(BF16)
         out_ref[block * 8 : block * 8 + 8, :] += dot(maps[block * 8 : block * 8 + 8], hidden[...])
     last = elapsed[tokens - 1 : tokens]
+    spare = send_ref.shape[2] - channels
+    parts = channels // spare
     last_high = last.astype(BF16).astype(F32)
-    line = iota((16, channels), 0)
-    ends = jnp.where(line == 0, last_high, jnp.where(line == 1, last - last_high, 0.0)).astype(BF16)
-    final = state.astype(BF16)
+    line = iota((states, spare), 0)
+    ends = jnp.zeros((states, spare), F32)
+    for part in range(parts):
+        high_part = last_high[:, part * spare : part * spare + spare]
+        rest_part = last[:, part * spare : part * spare + spare] - high_part
+        ends = jnp.where(line == part, high_part, ends)
+        ends = jnp.where(line == part + parts, rest_part, ends)
+    final = jnp.concatenate([state, ends], axis=1).astype(BF16)
     for peer in range(send_ref.shape[0]):
-        send_ref[peer, 0:states, :] = final
-        send_ref[peer, states : states + 16, :] = ends
+        send_ref[peer] = final
 
 
 def finish_body(me, in_ref, rate_ref, out_in_ref, elapsed_ref, map_ref, gate_ref, mixed_ref, carried):
@@ -214,10 +269,12 @@
     tokens = elapsed_ref.shape[0]
     rate = rate_ref[...] * (-LOG2E)
     state = jnp.zeros((states, channels), F32)
+    parts = channels // (in_ref.shape[2] - channels)
     for peer in range(in_ref.shape[0]):
-        ends = in_ref[peer, states : states + 16, :].astype(F32)
-        length = ends[0:1] + ends[1:2]
-        final = in_ref[peer, 0:states, :].astype(F32)
+        message = in_ref[peer].astype(F32)
+        final = message[:, :channels]
+        ends = message[:parts, channels:] + message[parts : 2 * parts, channels:]
+        length = jnp.concatenate([ends[part : part + 1] for part in range(parts)], axis=1)
         state = jnp.where(peer < me[0], jnp.exp2(length * rate) * state + final, state)
     corrected = []
     for block in range(tokens // 8):
@@ -250,13 +307,38 @@
     my_gain = lax.dynamic_slice_in_dim(norm_gain, lax.axis_index("chan") * features, features)
     my_gain = jnp.broadcast_to(my_gain[:, None], (features, row_count))
     weight = jnp.transpose(in_weight, (1, 2, 0)).reshape(2 * channels, width)
-    rate = decay_rate.T
-
-    pieces = call(
+    pieces, starts = call(
         functools.partial(pack_body, slots),
-        shape((peers * 16, features), BF16),
-        [SMEM, SMEM, VMEM, VMEM],
-        (group_target, me, tokens.T, starts),
+        (shape((peers * 16, features), BF16), shape((1, row_count), jnp.int32)),
+        [SMEM, HBM, HBM, HBM],
+        (me, in_hbm(group_target), in_hbm(tokens.T), in_hbm(starts)),
+        [
+            pltpu.SMEM((slots,), jnp.int32),
+            pltpu.VMEM((features, row_count), BF16),
+            pltpu.SemaphoreType.DMA((3,)),
+        ],
+    )
+    weight = in_hbm(weight)
+    sources = (proj_weight.T, dt_weight, decay_rate.T, conv_weight, conv_bias, dt_bias, skip_gain)
+    scan_weight, proj, dtw, rate, cols, rows = call(
+        fetch_body,
+        (
+            shape((channels, width), BF16),
+            shape((rank + 2 * states, channels), BF16),
+            shape((rank, channels), BF16),
+            shape((states, channels), F32),
+            shape((channels, 8), F32),
+            shape((8, channels), F32),
+        ),
+        [HBM] * 8,
+        (weight, *(in_hbm(source) for source in sources)),
+        [
+            pltpu.VMEM(conv_weight.shape, F32),
+            pltpu.VMEM((channels,), F32),
+            pltpu.VMEM((channels,), F32),
+            pltpu.VMEM((channels,), F32),
+            pltpu.SemaphoreType.DMA((8,)),
+        ],
     )
     arrived = lax.all_to_all(pieces.reshape(peers, 16, features), "dp", 0, 0, tiled=True)
     payload = call(
@@ -267,15 +349,19 @@
     )
     gathered = lax.all_gather(payload, "chan", axis=0)
     low, act, gate = call(
-        functools.partial(project_body, features),
+        functools.partial(project_body, features, conv_weight.shape[0]),
         (
             shape((rank + 2 * states, row_count), BF16),
             shape((channels, row_count), BF16),
             shape((channels, row_count), F32),
         ),
-        [VMEM] * 6,
-        (gathered, weight, conv_weight.T, conv_bias[:, None], proj_weight.T, starts),
-        [pltpu.VMEM((width, 2 * row_count), BF16)],
+        [VMEM, VMEM, HBM, VMEM, VMEM, VMEM],
+        (gathered, scan_weight, weight, cols, proj, starts),
+        [
+            pltpu.VMEM((width, 2 * row_count), BF16),
+            pltpu.VMEM((channels, width), BF16),
+            pltpu.SemaphoreType.DMA,
+        ],
     )
     lows = lax.all_gather(low, "chan", axis=0)
     out, elapsed, maps, send = call(
@@ -284,10 +370,10 @@
             shape((row_count, channels), F32),
             shape((row_count, channels), F32),
             shape((row_count, row_count), BF16),
-            shape((peers, states + 16, channels), BF16),
+            shape((peers, states, -(-channels // 128) * 128), BF16),
         ),
-        [VMEM] * 7,
-        (lows, act, dt_weight, dt_bias[None, :], rate, skip_gain[None, :], starts),
+        [VMEM] * 6,
+        (lows, act, dtw, rate, rows, starts),
         [
             pltpu.VMEM((row_count, channels), F32),
             pltpu.VMEM((row_count, channels), F32),

time: 102 us -> 91 us (0.89)
  local copies, waits for them, and re-layouts: 9.42 us -> 0.85 us
  blocking collectives: 64.3 us -> 57.2 us
  Pallas kernels: 6.3 us -> 10 us
  waiting for transfers between devices: 7.41 us -> 8.82 us
    all_to_all x1, blocking collectives: 25.2 us -> 18 us  [local(): ends = lax.all_to_all(send, 'dp', 0, 0, tiled=True)]
    unnamed x17 -> x0, local copies, waits for them, and re-layouts: 6.41 us -> none
    pallas_call x5 -> x6, Pallas kernels: 6.3 us -> 10 us  [call(): pl.pallas_call(body, out_shape=outs, in_specs=specs, out_specs=jax.tree.m...]
    broadcast_in_dim x3 -> x0, local copies, waits for them, and re-layouts: 2.15 us -> none  [the longest x1 0.78 us: local(): conv_bias[:, None]]
    all_to_all x1, waiting for transfers between devices: 7.41 us -> 8.82 us  [local(): lax.all_to_all(pieces.reshape(peers, 16, features), 'dp', 0, 0, tiled=True)]
  transfers between devices with their start and end apart: 1 -> 1, of which waited for: 1 -> 1; matrix products, arithmetic and copies ran while one was open for 4% -> 1% of each run, Pallas kernels for 0% -> 2%
where the time goes in v1:
time: 91 us; the launch traced here: 90.6 us
  blocking collectives  57.2 us (63%)
  starting transfers between devices  13.7 us (15%)
  Pallas kernels  10 us (11%)
  waiting for transfers between devices  8.82 us (10%)
    all_gather x1, blocking collectives, local(): gathered = lax.all_gather(payload, 'chan', axis=0)  22 us
    all_to_all x1, blocking collectives, local(): ends = lax.all_to_all(send, 'dp', 0, 0, tiled=True)  18 us
    all_gather x1, blocking collectives, local(): lows = lax.all_gather(low, 'chan', axis=0)  17.1 us
    all_to_all x1, starting transfers between devices, local(): lax.all_to_all(pieces.reshape(peers, 16, features), 'dp', 0, 0, tiled=True)  13.7 us
    pallas_call x6, Pallas kernels, call(): pl.pallas_call(body, out_shape=outs, in_specs=specs, out_specs=jax.tree.m...  10 us
    all_to_all x1, waiting for transfers between devices, local(): lax.all_to_all(pieces.reshape(peers, 16, features), 'dp', 0, 0, tiled=True)  8.82 us
  transfers between devices with their start and end apart: 1, of which 1 were waited for; matrix products, arithmetic and copies ran while one was open for 1% of the time, Pallas kernels for 2%

profile of v1, /device:TPU:1, one launch (start us, length us, event | category | flops | bytes accessed | tf_op | source)
XLA Modules:
  0.0 90.6 jit_solution(12605310773720170688)
XLA Ops:
  0.0 1.8 %shard_map.118 = (bf16[512,160]{1,0:T(8,128)(2,1)}, s32[1,128]{1,0:T(1,128)S(1)}) custom-call(s32[1]{0:T(128)} %bitcast.me, s32[16]{0:T(128)} %target_hbm.1, bf16[160,128]{1,0:T(8,128)(2,1)} %bitcast.19, s32[1,128]{1,0:T(1,128)} %bitcast.21), custom_call_target="tpu_custom_call" | custom-call | tf_op jit(solution)/shard_map/pallas_call | solution.py:39
  1.8 13.7 %all-to-all-start = ((bf16[32,16,160]{2,1,0:T(8,128)(2,1)}), bf16[32,16,160]{2,1,0:T(8,128)(2,1)S(1)}, u32[]{:S(2)}, u32[]{:S(2)}) async-start(bf16[32,16,160]{2,1,0:T(8,128)(2,1)} %bitcast.3), calls=%async_computation | async-start | bytes 524288 | tf_op jit(solution)/shard_map/all_to_all | solution.py:343
  15.5 0.8 dynamic_slice.3
  16.3 1.6 %shard_map.120 = (bf16[320,2560]{1,0:T(8,128)(2,1)S(1)}, bf16[192,320]{1,0:T(8,128)(2,1)S(1)}, bf16[160,320]{1,0:T(8,128)(2,1)S(1)}, f32[16,320]{1,0:T(8,128)S(1...) custom-call(bf16[640,2560]{1,0:T(8,128)(2,1)} %bitcast.16, bf16[192,320]{1,0:T(8,128)(2,1)} %bitcast.18, ...), custom_call_target="tpu_custom_call" | custom-call | tf_op jit(solution)/shard_map/pallas_call | solution.py:39
  17.9 8.8 %all-to-all-done = bf16[32,16,160]{2,1,0:T(8,128)(2,1)S(1)} async-done(((bf16[32,16,160]{2,1,0:T(8,128)(2,1)}), bf16[32,16,160]{2,1,0:T(8,128)(2,1)S(1)}, u32[]{:S(2)}, u32[]{:S(2)}) %all-to-all-start) | async-done | bytes 163872 | tf_op jit(solution)/shard_map/all_to_all | solution.py:343
  26.7 0.1 broadcast_in_dim.2.gain_ref
  26.8 0.3 shard_map.119
  27.1 22.0 %all-gather = bf16[3072,128]{1,0:T(8,128)(2,1)S(1)} all-gather(bf16[192,128]{1,0:T(8,128)(2,1)S(1)} %shard_map.119), channel_id=2, replica_groups=mesh['dp'=32,'chan'=16] {'chan'}, dimensions={0}, use_global_device_ids=true | all-gather | bytes 835584 | tf_op jit(solution)/shard_map/all_gather | solution.py:350
  49.1 3.1 %shard_map.121 = (bf16[192,128]{1,0:T(8,128)(2,1)S(1)}, bf16[320,128]{1,0:T(8,128)(2,1)S(1)}, f32[320,128]{1,0:T(8,128)S(1)}) custom-call(bf16[16,192,128]{2,1,0:T(8,128)(2,1)S(1)} %bitcast.13, bf16[320,2560]{1,0:T(8,128)(2,1)S(1)} %get-tuple-element.21.weight_ref, bf16[640,2560]{1,0:T(8,128)(2,1)} %bitcast.17, f32[320,8]{1,0:T(8,128)S(1)} %get-tuple-element.22.taps_ref, ...), custom_call_target="tpu_custom_call" | custom-call | tf_op jit(solution)/shard_map/pallas_call | solution.py:39
  52.3 17.1 %all-gather.1 = bf16[3072,128]{1,0:T(8,128)(2,1)S(1)} all-gather(bf16[192,128]{1,0:T(8,128)(2,1)S(1)} %get-tuple-element.25), channel_id=3, replica_groups=mesh['dp'=32,'chan'=16] {'chan'}, dimensions={0}, use_global_device_ids=true | all-gather | bytes 835584 | tf_op jit(solution)/shard_map/all_gather | solution.py:366
  69.4 1.5 %shard_map.122 = (f32[128,320]{1,0:T(8,128)S(1)}, f32[128,320]{1,0:T(8,128)S(1)}, bf16[128,128]{1,0:T(8,128)(2,1)S(1)}, bf16[32,16,384]{2,1,0:T(8,128)(2,1)S(1)}) custom-call(bf16[16,192,128]{2,1,0:T(8,128)(2,1)S(1)} %bitcast.14, bf16[320,128]{1,0:T(8,128)(2,1)S(1)} %get-tuple-element.26.act_ref, bf16[160,320]{1,0:T(8,128)(2,1)S(1)} %get-tuple-element.27.dtw_ref, ...), custom_call_target="tpu_custom_call" | custom-call | tf_op jit(solution)/shard_map/pallas_call | solution.py:39
  70.9 18.0 %all_to_all.10.in_ref = bf16[32,16,384]{2,1,0:T(8,128)(2,1)S(1)} all-to-all(bf16[32,16,384]{2,1,0:T(8,128)(2,1)S(1)} %get-tuple-element.30), channel_id=1, replica_groups=mesh['dp'=32,'chan'=16] {'dp'}, dimensions={0} | all-to-all | bytes 786432 | tf_op jit(solution)/shard_map/all_to_all | solution.py:383
  88.9 1.7 %shard_map.123 = bf16[320,128]{1,0:T(8,128)(2,1)} custom-call(s32[1]{0:T(128)} %bitcast.me, bf16[32,16,384]{2,1,0:T(8,128)(2,1)S(1)} %all_to_all.10.in_ref, f32[16,320]{1,0:T(8,128)S(1)} %get-tuple-element.28.rate_ref, f32[128,320]{1,0:T(8,128)S(1)} %get-tuple-element.31.out_in_ref, f32[128,320]{1,0:T(8,128)S(1)} %get-tuple-element.32.elapsed_ref, ...), custom_call_target="tpu_custom_call" | custom-call | tf_op jit(solution)/shard_map/pallas_call | solution.py:39
Async XLA Ops:
  1.8 24.9 %all-to-all-start = ((bf16[32,16,160]{2,1,0:T(8,128)(2,1)}), bf16[32,16,160]{2,1,0:T(8,128)(2,1)S(1)}, u32[]{:S(2)}, u32[]{:S(2)}) async-start(bf16[32,16,160]{2,1,0:T(8,128)(2,1)} %bitcast.3), calls=%async_computation | async-start | bytes 524288 | tf_op jit(solution)/shard_map/all_to_all | solution.py:343

commit v2 on v1

--- a/solution.py
+++ b/solution.py
@@ -164,14 +164,11 @@
 
 
 def project_body(
-    features, taps, in_ref, weight_ref, weight_hbm, taps_ref, proj_ref, starts_ref,
-    low_ref, act_ref, gate_ref, wide, gate_weight, sem,
+    features, taps, in_ref, weight_ref, taps_ref, proj_ref, starts_ref, low_ref, act_ref, wide,
 ):
     count = in_ref.shape[0]
     tokens = in_ref.shape[2]
     channels = act_ref.shape[0]
-    fetch = pltpu.make_async_copy(weight_hbm.at[channels:], gate_weight, sem)
-    fetch.start()
     width = count * features
     sums = jnp.zeros((16, tokens), F32)
     for peer in range(count):
@@ -202,15 +199,11 @@
     act = (convolved * (1.0 / (1.0 + jnp.exp(-convolved)))).astype(BF16)
     act_ref[...] = act
     low_ref[...] = dot(proj_ref[...], act).astype(BF16)
-    fetch.wait()
-    gate = dot(gate_weight[...], wide[:, 0:tokens])
-    gate = (gate * scale_main).astype(BF16).astype(F32)
-    gate_ref[...] = gate * (1.0 / (1.0 + jnp.exp(-gate)))
-
-
-def scan_body(
+
+
+def state_body(
     rank, in_ref, act_ref, dtw_ref, rate_ref, rows_ref, starts_ref,
-    out_ref, elapsed_ref, map_ref, send_ref, decay_step, drive_step, hidden,
+    send_ref, decay_step, drive_step, maps_ref,
 ):
     tokens = in_ref.shape[2]
     states, channels = rate_ref.shape
@@ -219,36 +212,19 @@
         low = low + in_ref[peer].astype(F32)
     dt_low = low[:rank].astype(BF16)
     in_map = low[rank : rank + states]
-    out_map = low[rank + states :]
+    maps_ref[...] = low[rank:]
     raw = dot(dt_low, dtw_ref[...], TN) + rows_ref[0:1, :]
     step = jnp.maximum(raw, 0.0) + jnp.log1p(jnp.exp(-jnp.abs(raw)))
-    act = jnp.transpose(act_ref[...].astype(F32))
-    out_ref[...] = rows_ref[1:2, :] * act
-    drive_step[...] = step * act
+    drive_step[...] = step * jnp.transpose(act_ref[...].astype(F32))
     first = jnp.transpose(jnp.broadcast_to(starts_ref[...].astype(F32), (tokens, tokens)))
-    first = first[:, :1]
-    step = jnp.where(first > 0.5, FAR, step)
+    step = jnp.where(first[:, :1] > 0.5, FAR, step)
     decay_step[...] = step
-    high = step.astype(BF16)
-    rest = (step - high.astype(F32)).astype(BF16)
-    lower = jnp.where(iota((tokens, tokens), 0) >= iota((tokens, tokens), 1), 1.0, 0.0).astype(BF16)
-    elapsed = dot(lower, high) + dot(lower, rest)
-    elapsed_ref[...] = elapsed
-    spread = jnp.where((iota((states, tokens), 1) & (states - 1)) == iota((states, tokens), 0), 1.0, 0.0)
-    maps = dot(out_map.astype(BF16), spread.astype(BF16), TN)
-    own = (iota((tokens, tokens), 1) // states) == (iota((tokens, tokens), 0) & 7)
-    maps = jnp.where(own, maps, 0.0).astype(BF16)
-    map_ref[...] = maps
+    last = jnp.sum(step, axis=0, keepdims=True)
     rate = rate_ref[...] * (-LOG2E)
     state = jnp.zeros((states, channels), F32)
-    for block in range(tokens // 8):
-        for inner in range(8):
-            t = block * 8 + inner
-            decay = jnp.exp2(decay_step[t : t + 1, :] * rate)
-            state = decay * state + drive_step[t : t + 1, :] * in_map[:, t : t + 1]
-            hidden[inner * states : (inner + 1) * states, :] = state.astype(BF16)
-        out_ref[block * 8 : block * 8 + 8, :] += dot(maps[block * 8 : block * 8 + 8], hidden[...])
-    last = elapsed[tokens - 1 : tokens]
+    for t in range(tokens):
+        decay = jnp.exp2(decay_step[t : t + 1, :] * rate)
+        state = decay * state + drive_step[t : t + 1, :] * in_map[:, t : t + 1]
     spare = send_ref.shape[2] - channels
     parts = channels // spare
     last_high = last.astype(BF16).astype(F32)
@@ -262,6 +238,48 @@
     final = jnp.concatenate([state, ends], axis=1).astype(BF16)
     for peer in range(send_ref.shape[0]):
         send_ref[peer] = final
+
+
+def side_body(
+    features, in_ref, weight_hbm, act_ref, rate_ref, rows_ref, decay_step, drive_step, maps_ref,
+    out_ref, elapsed_ref, map_ref, gate_ref, wide, gate_weight, hidden, sem,
+):
+    count = in_ref.shape[0]
+    tokens = in_ref.shape[2]
+    states, channels = rate_ref.shape
+    fetch = pltpu.make_async_copy(weight_hbm.at[channels:], gate_weight, sem)
+    fetch.start()
+    sums = jnp.zeros((16, tokens), F32)
+    for peer in range(count):
+        wide[peer * features : (peer + 1) * features, :] = in_ref[peer, 0:features, :]
+        sums = sums + in_ref[peer, features + 16 : features + 32, :].astype(F32)
+    scale = lax.rsqrt((sums[0:1] + sums[1:2]) / (count * features) + EPSILON)
+    in_map = maps_ref[0:states, :]
+    out_map = maps_ref[states:, :]
+    step = decay_step[...]
+    high = step.astype(BF16)
+    rest = (step - high.astype(F32)).astype(BF16)
+    lower = jnp.where(iota((tokens, tokens), 0) >= iota((tokens, tokens), 1), 1.0, 0.0).astype(BF16)
+    elapsed_ref[...] = dot(lower, high) + dot(lower, rest)
+    spread = jnp.where((iota((states, tokens), 1) & (states - 1)) == iota((states, tokens), 0), 1.0, 0.0)
+    maps = dot(out_map.astype(BF16), spread.astype(BF16), TN)
+    own = (iota((tokens, tokens), 1) // states) == (iota((tokens, tokens), 0) & 7)
+    maps = jnp.where(own, maps, 0.0).astype(BF16)
+    map_ref[...] = maps
+    out_ref[...] = rows_ref[1:2, :] * jnp.transpose(act_ref[...].astype(F32))
+    rate = rate_ref[...] * (-LOG2E)
+    state = jnp.zeros((states, channels), F32)
+    for block in range(tokens // 8):
+        for inner in range(8):
+            t = block * 8 + inner
+            decay = jnp.exp2(decay_step[t : t + 1, :] * rate)
+            state = decay * state + drive_step[t : t + 1, :] * in_map[:, t : t + 1]
+            hidden[inner * states : (inner + 1) * states, :] = state.astype(BF16)
+        out_ref[block * 8 : block * 8 + 8, :] += dot(maps[block * 8 : block * 8 + 8], hidden[...])
+    fetch.wait()
+    gate = dot(gate_weight[...], wide[...])
+    gate = (gate * scale).astype(BF16).astype(F32)
+    gate_ref[...] = gate * (1.0 / (1.0 + jnp.exp(-gate)))
 
 
 def finish_body(me, in_ref, rate_ref, out_in_ref, elapsed_ref, map_ref, gate_ref, mixed_ref, carried):
@@ -348,36 +366,36 @@
         (arrived.reshape(peers * 16, features), my_gain),
     )
     gathered = lax.all_gather(payload, "chan", axis=0)
-    low, act, gate = call(
+    low, act = call(
         functools.partial(project_body, features, conv_weight.shape[0]),
+        (shape((rank + 2 * states, row_count), BF16), shape((channels, row_count), BF16)),
+        [VMEM] * 5,
+        (gathered, scan_weight, cols, proj, starts),
+        [pltpu.VMEM((width, 2 * row_count), BF16)],
+    )
+    lows = lax.all_gather(low, "chan", axis=0)
+    by_token = shape((row_count, channels), F32)
+    send, decay_step, drive_step, maps = call(
+        functools.partial(state_body, rank),
         (
-            shape((rank + 2 * states, row_count), BF16),
-            shape((channels, row_count), BF16),
-            shape((channels, row_count), F32),
-        ),
-        [VMEM, VMEM, HBM, VMEM, VMEM, VMEM],
-        (gathered, scan_weight, weight, cols, proj, starts),
-        [
-            pltpu.VMEM((width, 2 * row_count), BF16),
-            pltpu.VMEM((channels, width), BF16),
-            pltpu.SemaphoreType.DMA,
-        ],
-    )
-    lows = lax.all_gather(low, "chan", axis=0)
-    out, elapsed, maps, send = call(
-        functools.partial(scan_body, rank),
-        (
-            shape((row_count, channels), F32),
-            shape((row_count, channels), F32),
-            shape((row_count, row_count), BF16),
             shape((peers, states, -(-channels // 128) * 128), BF16),
+            by_token,
+            by_token,
+            shape((2 * states, row_count), F32),
         ),
         [VMEM] * 6,
         (lows, act, dtw, rate, rows, starts),
+    )
+    out, elapsed, own_maps, gate = call(
+        functools.partial(side_body, features),
+        (by_token, by_token, shape((row_count, row_count), BF16), shape((channels, row_count), F32)),
+        [VMEM, HBM] + [VMEM] * 6,
+        (gathered, weight, act, rate, rows, decay_step, drive_step, maps),
         [
-            pltpu.VMEM((row_count, channels), F32),
-            pltpu.VMEM((row_count, channels), F32),
+            pltpu.VMEM((width, row_count), BF16),
+            pltpu.VMEM((channels, width), BF16),
             pltpu.VMEM((8 * states, channels), BF16),
+            pltpu.SemaphoreType.DMA,
         ],
     )
     ends = lax.all_to_all(send, "dp", 0, 0, tiled=True)
@@ -385,7 +403,7 @@
         finish_body,
         shape((channels, row_count), BF16),
         [SMEM] + [VMEM] * 6,
-        (me, ends, rate, out, elapsed, maps, gate),
+        (me, ends, rate, out, elapsed, own_maps, gate),
         [pltpu.VMEM((8 * states, channels), BF16)],
     )
     return mixed.T

time: 91 us -> 89.7 us (0.986)
  blocking collectives: 57.2 us -> 39.1 us
  waiting for transfers between devices: 8.82 us -> 20.3 us
  starting transfers between devices: 13.7 us -> 17.6 us
  Pallas kernels: 10 us -> 11.3 us
    all_to_all x1 -> x0, blocking collectives: 18 us -> none  [local(): ends = lax.all_to_all(send, 'dp', 0, 0, tiled=True)]
    all_to_all x0 -> x1, waiting for transfers between devices: none -> 11.4 us  [local(): ends = lax.all_to_all(send, 'dp', 0, 0, tiled=True)]
    all_to_all x0 -> x1, starting transfers between devices: none -> 3.88 us  [local(): ends = lax.all_to_all(send, 'dp', 0, 0, tiled=True)]
    pallas_call x6 -> x7, Pallas kernels: 10 us -> 11.3 us  [call(): pl.pallas_call(body, out_shape=outs, in_specs=specs, out_specs=jax.tree.m...]
  transfers between devices with their start and end apart: 1 -> 2, of which waited for: 1 -> 2; matrix products, arithmetic and copies ran while one was open for 1% -> 1% of each run, Pallas kernels for 2% -> 5%
where the time goes in v2:
time: 89.7 us; the launch traced here: 89.2 us
  blocking collectives  39.1 us (44%)
  waiting for transfers between devices  20.3 us (23%)
  starting transfers between devices  17.6 us (20%)
  Pallas kernels  11.3 us (13%)
    all_gather x1, blocking collectives, local(): gathered = lax.all_gather(payload, 'chan', axis=0)  22 us
    all_gather x1, blocking collectives, local(): lows = lax.all_gather(low, 'chan', axis=0)  17.1 us
    all_to_all x1, starting transfers between devices, local(): lax.all_to_all(pieces.reshape(peers, 16, features), 'dp', 0, 0, tiled=True)  13.7 us
    all_to_all x1, waiting for transfers between devices, local(): ends = lax.all_to_all(send, 'dp', 0, 0, tiled=True)  11.4 us
    pallas_call x7, Pallas kernels, call(): pl.pallas_call(body, out_shape=outs, in_specs=specs, out_specs=jax.tree.m...  11.3 us
    all_to_all x1, waiting for transfers between devices, local(): lax.all_to_all(pieces.reshape(peers, 16, features), 'dp', 0, 0, tiled=True)  8.82 us
    all_to_all x1, starting transfers between devices, local(): ends = lax.all_to_all(send, 'dp', 0, 0, tiled=True)  3.88 us
  transfers between devices with their start and end apart: 2, of which 2 were waited for; matrix products, arithmetic and copies ran while one was open for 1% of the time, Pallas kernels for 5%

profile of v2, /device:TPU:1, one launch (start us, length us, event | category | flops | bytes accessed | tf_op | source)
XLA Modules:
  0.0 89.2 jit_solution(2956329204200542883)
XLA Ops:
  0.0 1.8 %shard_map.118 = (bf16[512,160]{1,0:T(8,128)(2,1)}, s32[1,128]{1,0:T(1,128)S(1)}) custom-call(s32[1]{0:T(128)} %bitcast.me, s32[16]{0:T(128)} %target_hbm.1, bf16[160,128]{1,0:T(8,128)(2,1)} %bitcast.20, s32[1,128]{1,0:T(1,128)} %bitcast.22), custom_call_target="tpu_custom_call" | custom-call | tf_op jit(solution)/shard_map/pallas_call | solution.py:39
  1.8 13.7 %all-to-all-start = ((bf16[32,16,160]{2,1,0:T(8,128)(2,1)}), bf16[32,16,160]{2,1,0:T(8,128)(2,1)S(1)}, u32[]{:S(2)}, u32[]{:S(2)}) async-start(bf16[32,16,160]{2,1,0:T(8,128)(2,1)} %bitcast.3), calls=%async_computation | async-start | bytes 524288 | tf_op jit(solution)/shard_map/all_to_all | solution.py:361
  15.5 0.8 dynamic_slice.3
  16.3 1.6 %shard_map.120 = (bf16[320,2560]{1,0:T(8,128)(2,1)S(1)}, bf16[192,320]{1,0:T(8,128)(2,1)S(1)}, bf16[160,320]{1,0:T(8,128)(2,1)S(1)}, f32[16,320]{1,0:T(8,128)S(1...) custom-call(bf16[640,2560]{1,0:T(8,128)(2,1)} %bitcast.17, bf16[192,320]{1,0:T(8,128)(2,1)} %bitcast.19, ...), custom_call_target="tpu_custom_call" | custom-call | tf_op jit(solution)/shard_map/pallas_call | solution.py:39
  17.9 8.8 %all-to-all-done = bf16[32,16,160]{2,1,0:T(8,128)(2,1)S(1)} async-done(((bf16[32,16,160]{2,1,0:T(8,128)(2,1)}), bf16[32,16,160]{2,1,0:T(8,128)(2,1)S(1)}, u32[]{:S(2)}, u32[]{:S(2)}) %all-to-all-start) | async-done | bytes 163872 | tf_op jit(solution)/shard_map/all_to_all | solution.py:361
  26.7 0.1 broadcast_in_dim.2.gain_ref
  26.8 0.3 shard_map.119
  27.1 22.0 %all-gather = bf16[3072,128]{1,0:T(8,128)(2,1)S(1)} all-gather(bf16[192,128]{1,0:T(8,128)(2,1)S(1)} %shard_map.119), channel_id=2, replica_groups=mesh['dp'=32,'chan'=16] {'chan'}, dimensions={0}, use_global_device_ids=true | all-gather | bytes 835584 | tf_op jit(solution)/shard_map/all_gather | solution.py:368
  49.1 1.0 %shard_map.121 = (bf16[192,128]{1,0:T(8,128)(2,1)S(1)}, bf16[320,128]{1,0:T(8,128)(2,1)S(1)}) custom-call(bf16[16,192,128]{2,1,0:T(8,128)(2,1)S(1)} %bitcast.13, bf16[320,2560]{1,0:T(8,128)(2,1)S(1)} %get-tuple-element.24.weight_ref, f32[320,8]{1,0:T(8,128)S(1)} %get-tuple-element.25.taps_ref, bf16[192,320]{1,0:T(8,128)(2,1)S(1)} %get-tuple-element.26.proj_ref, ...), custom_call_target="tpu_custom_call" | custom-call | tf_op jit(solution)/shard_map/pallas_call | solution.py:39
  50.2 17.1 %all-gather.1 = bf16[3072,128]{1,0:T(8,128)(2,1)S(1)} all-gather(bf16[192,128]{1,0:T(8,128)(2,1)S(1)} %get-tuple-element.28), channel_id=3, replica_groups=mesh['dp'=32,'chan'=16] {'chan'}, dimensions={0}, use_global_device_ids=true | all-gather | bytes 835584 | tf_op jit(solution)/shard_map/all_gather | solution.py:376
  67.2 1.9 %shard_map.122 = (bf16[32,16,384]{2,1,0:T(8,128)(2,1)}, f32[128,320]{1,0:T(8,128)S(1)}, f32[128,320]{1,0:T(8,128)S(1)}, f32[32,128]{1,0:T(8,128)S(1)}) custom-call(bf16[16,192,128]{2,1,0:T(8,128)(2,1)S(1)} %bitcast.15, bf16[320,128]{1,0:T(8,128)(2,1)S(1)} %get-tuple-element.29.act_ref, bf16[160,320]{1,0:T(8,128)(2,1)S(1)} %get-tuple-element.30.dtw_ref, ...), custom_call_target="tpu_custom_call" | custom-call | tf_op jit(solution)/shard_map/pallas_call | solution.py:39
  69.2 3.9 %all-to-all-start.1 = ((bf16[32,16,384]{2,1,0:T(8,128)(2,1)}), bf16[32,16,384]{2,1,0:T(8,128)(2,1)S(1)}, u32[]{:S(2)}, u32[]{:S(2)}) async-start(bf16[32,16,384]{2,1,0:T(8,128)(2,1)} %get-tuple-element.33), calls=%async_computation.1 | async-start | bytes 786432 | tf_op jit(solution)/shard_map/all_to_all | solution.py:401
  73.1 3.0 %shard_map.123 = (f32[128,320]{1,0:T(8,128)S(1)}, f32[128,320]{1,0:T(8,128)S(1)}, bf16[128,128]{1,0:T(8,128)(2,1)S(1)}, f32[320,128]{1,0:T(8,128)S(1)}) custom-call(bf16[16,192,128]{2,1,0:T(8,128)(2,1)S(1)} %bitcast.14, bf16[640,2560]{1,0:T(8,128)(2,1)} %bitcast.18, bf16[320,128]{1,0:T(8,128)(2,1)S(1)} %get-tuple-element.29.act_ref, ...), custom_call_target="tpu_custom_call" | custom-call | tf_op jit(solution)/shard_map/pallas_call | solution.py:39
  76.1 11.4 %all-to-all-done.1.in_ref = bf16[32,16,384]{2,1,0:T(8,128)(2,1)S(1)} async-done(((bf16[32,16,384]{2,1,0:T(8,128)(2,1)}), bf16[32,16,384]{2,1,0:T(8,128)(2,1)S(1)}, u32[]{:S(2)}, u32[]{:S(2)}) %all-to-all-start.1) | async-done | bytes 393248 | tf_op jit(solution)/shard_map/all_to_all | solution.py:401
  87.5 1.7 %shard_map.124 = bf16[320,128]{1,0:T(8,128)(2,1)} custom-call(s32[1]{0:T(128)} %bitcast.me, bf16[32,16,384]{2,1,0:T(8,128)(2,1)S(1)} %all-to-all-done.1.in_ref, f32[16,320]{1,0:T(8,128)S(1)} %get-tuple-element.31.rate_ref, f32[128,320]{1,0:T(8,128)S(1)} %get-tuple-element.37.out_in_ref, f32[128,320]{1,0:T(8,128)S(1)} %get-tuple-element.38.elapsed_ref, ...), custom_call_target="tpu_custom_call" | custom-call | tf_op jit(solution)/shard_map/pallas_call | solution.py:39
Async XLA Ops:
  1.8 24.9 %all-to-all-start = ((bf16[32,16,160]{2,1,0:T(8,128)(2,1)}), bf16[32,16,160]{2,1,0:T(8,128)(2,1)S(1)}, u32[]{:S(2)}, u32[]{:S(2)}) async-start(bf16[32,16,160]{2,1,0:T(8,128)(2,1)} %bitcast.3), calls=%async_computation | async-start | bytes 524288 | tf_op jit(solution)/shard_map/all_to_all | solution.py:361
  69.2 18.4 %all-to-all-start.1 = ((bf16[32,16,384]{2,1,0:T(8,128)(2,1)}), bf16[32,16,384]{2,1,0:T(8,128)(2,1)S(1)}, u32[]{:S(2)}, u32[]{:S(2)}) async-start(bf16[32,16,384]{2,1,0:T(8,128)(2,1)} %get-tuple-element.33), calls=%async_computation.1 | async-start | bytes 786432 | tf_op jit(solution)/shard_map/all_to_all | solution.py:401

commit v3 on v2

--- a/solution.py
+++ b/solution.py
@@ -46,46 +46,55 @@
     )(*args)
 
 
-def pack_body(slots, me, target_hbm, tok_hbm, starts_hbm, out_ref, starts_ref, target, tok_ref, sems):
+def pack_body(slots, me, target_hbm, tok_hbm, starts_hbm, out_ref, starts_ref, target, tok_ref, pieces, sems):
     copies = [
         pltpu.make_async_copy(target_hbm, target, sems.at[0]),
-        pltpu.make_async_copy(tok_hbm, tok_ref, sems.at[1]),
-        pltpu.make_async_copy(starts_hbm, starts_ref, sems.at[2]),
+        pltpu.make_async_copy(starts_hbm, starts_ref, sems.at[1]),
+        pltpu.make_async_copy(tok_hbm, tok_ref, sems.at[2]),
     ]
     for copy in copies:
         copy.start()
-    for copy in copies:
-        copy.wait()
     features, tokens = tok_ref.shape
-    rows = out_ref.shape[0]
-    lane = iota((1, tokens), 1)
-    where_to = jnp.zeros((1, tokens), jnp.int32)
+    peers = pieces.shape[0]
+    parts = features // 16
+    pieces[...] = jnp.zeros(pieces.shape, F32)
+    lane = iota((16, tokens), 1)
+    source = iota((tokens, tokens), 0)
+    place = iota((tokens, tokens), 1)
+    late = (source < features // 2) & ((source & 7) >= 5)
+    to_tail = jnp.where(
+        late & (place == features // 2 + 3 * (source >> 3) + (source & 7) - 5), 1.0, 0.0
+    ).astype(BF16)
+    copies[2].wait()
+    slabs = [tok_ref[16 * part : 16 * part + 16, :].astype(F32) for part in range(parts)]
+    groups = []
     for group in range(slots):
-        where_to = jnp.where((lane >> 3) == group, target[group], where_to)
-    dev = where_to // slots
-    slot = where_to % slots
-    inner = lane & 7
-    main_key = dev * 16 + inner
-    tail_key = jnp.where((slot == slots - 1) & (inner >= 5), (dev + 1) * 16 + inner + 3, -1)
-    slot_key = jnp.where(inner == 0, dev * 16 + 11, -1)
-    row = iota((rows, tokens), 0)
-    pick = jnp.where((row == main_key) | (row == tail_key), 1.0, 0.0)
-    mark = jnp.where(row == slot_key, (slot + 1).astype(F32), 0.0)
-    both = jnp.concatenate([pick, mark], axis=1).astype(BF16)
-    values = jnp.concatenate([tok_ref[...], jnp.ones((features, tokens), BF16)], axis=1)
-    pieces = dot(both, values, NT)
-    fresh = 1.0 - jnp.broadcast_to(starts_ref[...].astype(F32), (8, tokens))
-    lane8 = iota((8, tokens), 1)
-    next_one = pltpu.roll(fresh, tokens - 1, 1)
-    next_two = pltpu.roll(fresh, tokens - 2, 1)
-    open_tail = jnp.where(
-        lane8 == tokens - 1, 1.0, jnp.where(lane8 == tokens - 2, next_one, next_one * next_two)
-    )
-    open_tail = jnp.where(lane8 >= tokens - 3, open_tail, 0.0)[:1]
-    open_wide = jnp.concatenate([open_tail, jnp.zeros((1, features - tokens), F32)], axis=1)
-    row_wide = iota((rows, features), 0)
-    pieces = jnp.where(row_wide == (me[0] + 1) * 16 + 12, open_wide, pieces)
-    out_ref[...] = pieces.astype(BF16)
+        piece = jnp.zeros((16, tokens), F32)
+        for part in range(parts):
+            shift = (8 * (part - group)) % tokens
+            moved = slabs[part] if shift == 0 else pltpu.roll(slabs[part], shift, 1)
+            piece = jnp.where((lane >> 3) == part, moved, piece)
+        groups.append(piece)
+    tails = dot(jnp.concatenate(groups, axis=0).astype(BF16), to_tail)
+    copies[0].wait()
+    copies[1].wait()
+    fresh = 1.0 - jnp.broadcast_to(starts_ref[...].astype(F32), (16, tokens))
+    one = pltpu.roll(fresh, (114 - (tokens - 1)) % tokens, 1)
+    two = pltpu.roll(fresh, (113 - (tokens - 1)) % tokens, 1)
+    flags = jnp.where(
+        lane == 115, 1.0, jnp.where(lane == 114, one, jnp.where(lane == 113, one * two, 0.0))
+    )
+    after = me[0] + 1
+    pieces[jnp.minimum(after, peers - 1)] += jnp.where(after < peers, flags, 0.0)
+    for group in range(slots):
+        dev = target[group] // slots
+        slot = target[group] % slots
+        label = jnp.where(lane == 112, (slot + 1).astype(F32), 0.0)
+        pieces[dev] += groups[group] + label
+        follows = (slot == slots - 1) & (dev + 1 < peers)
+        tail = jnp.where(follows, tails[16 * group : 16 * group + 16], 0.0)
+        pieces[jnp.minimum(dev + 1, peers - 1)] += tail
+    out_ref[...] = pieces[...].astype(BF16)
 
 
 def fetch_body(
@@ -122,23 +131,34 @@
 
 
 def place_body(in_ref, gain_ref, out_ref):
-    rows, features = in_ref.shape
-    tokens = out_ref.shape[1]
-    arrived = in_ref[...]
-    head = arrived[:, :tokens].astype(F32).reshape(rows // 16, 16, tokens)
-    label = jnp.broadcast_to(head[:, 11:12, :], head.shape).reshape(rows, tokens)
-    open_tail = jnp.sum(head, axis=0)[12:13]
-    row = (iota((rows, tokens), 0) & 15).astype(F32)
-    lane = iota((rows, tokens), 1)
-    want = (((lane >> 3) + 1) * 16 + (lane & 7)).astype(F32)
-    main = jnp.where(label * 16.0 + row == want, 1.0, 0.0)
-    tail_row = jnp.where(lane >= tokens - 3, lane - (tokens - 3) + 8, -1).astype(F32)
-    tail = jnp.where(row == tail_row, 1.0, 0.0)
-    pick = jnp.concatenate([main, tail], axis=1).astype(BF16)
-    found = dot(arrived, pick, TN)
+    peers, _, tokens = in_ref.shape
+    features = gain_ref.shape[0]
+    rows = 16 * peers
+    slots = tokens // 8
+    parts = features // 16
+    arrived = in_ref[...].reshape(rows, tokens)
+    wide = arrived.astype(F32)
+    label = jnp.broadcast_to(wide[:, 112:113], (rows, 16 * slots))
+    key = (iota((rows, 16 * slots), 1) + 16 - (iota((rows, 16 * slots), 0) & 15)).astype(F32)
+    pick = jnp.where(label * 16.0 == key, 1.0, 0.0).astype(BF16)
+    ordered = dot(pick, arrived, TN)
+    total = jnp.sum(wide.reshape(peers, 16, tokens), axis=0)
+    lane = iota((16, tokens), 1)
+    open_tail = jnp.where(lane >= tokens - 3, pltpu.roll(total, tokens - 3 - 113, 1), 0.0)
+    mains, tails = [], []
+    for part in range(parts):
+        slab = jnp.zeros((16, tokens), F32)
+        for slot in range(slots):
+            shift = (8 * (slot - part)) % tokens
+            piece = ordered[16 * slot : 16 * slot + 16]
+            moved = piece if shift == 0 else pltpu.roll(piece, shift, 1)
+            slab = jnp.where((lane >> 3) == slot, moved, slab)
+        mains.append(slab)
+        shift = (tokens - 3 - features // 2 - 3 * part) % tokens
+        tails.append((total if shift == 0 else pltpu.roll(total, shift, 1)) * open_tail)
+    x_main = jnp.concatenate(mains, axis=0)
+    x_tail = jnp.concatenate(tails, axis=0)
     gain = gain_ref[...]
-    x_main = found[:, :tokens]
-    x_tail = found[:, tokens:] * open_tail
     main_sq = jnp.sum(x_main * x_main, axis=0, keepdims=True)
     tail_sq = jnp.sum(x_tail * x_tail, axis=0, keepdims=True)
     out_ref[0:features, :] = (x_main * gain).astype(BF16)
@@ -242,7 +262,7 @@
 
 def side_body(
     features, in_ref, weight_hbm, act_ref, rate_ref, rows_ref, decay_step, drive_step, maps_ref,
-    out_ref, elapsed_ref, map_ref, gate_ref, wide, gate_weight, hidden, sem,
+    out_ref, share_ref, wide, gate_weight, hidden, gate_token, sem,
 ):
     count = in_ref.shape[0]
     tokens = in_ref.shape[2]
@@ -260,14 +280,21 @@
     high = step.astype(BF16)
     rest = (step - high.astype(F32)).astype(BF16)
     lower = jnp.where(iota((tokens, tokens), 0) >= iota((tokens, tokens), 1), 1.0, 0.0).astype(BF16)
-    elapsed_ref[...] = dot(lower, high) + dot(lower, rest)
+    elapsed = dot(lower, high) + dot(lower, rest)
     spread = jnp.where((iota((states, tokens), 1) & (states - 1)) == iota((states, tokens), 0), 1.0, 0.0)
     maps = dot(out_map.astype(BF16), spread.astype(BF16), TN)
     own = (iota((tokens, tokens), 1) // states) == (iota((tokens, tokens), 0) & 7)
     maps = jnp.where(own, maps, 0.0).astype(BF16)
-    map_ref[...] = maps
     out_ref[...] = rows_ref[1:2, :] * jnp.transpose(act_ref[...].astype(F32))
+    fetch.wait()
+    gate = dot(gate_weight[...], wide[...])
+    gate = (gate * scale).astype(BF16).astype(F32)
+    gate_token[...] = jnp.transpose(gate * (1.0 / (1.0 + jnp.exp(-gate))))
     rate = rate_ref[...] * (-LOG2E)
+    by_token = jnp.transpose(out_map)
+    for index in range(states):
+        remains = jnp.exp2(elapsed * rate[index : index + 1, :]) * gate_token[...]
+        share_ref[index] = (by_token[:, index : index + 1] * remains).astype(BF16)
     state = jnp.zeros((states, channels), F32)
     for block in range(tokens // 8):
         for inner in range(8):
@@ -276,36 +303,26 @@
             state = decay * state + drive_step[t : t + 1, :] * in_map[:, t : t + 1]
             hidden[inner * states : (inner + 1) * states, :] = state.astype(BF16)
         out_ref[block * 8 : block * 8 + 8, :] += dot(maps[block * 8 : block * 8 + 8], hidden[...])
-    fetch.wait()
-    gate = dot(gate_weight[...], wide[...])
-    gate = (gate * scale).astype(BF16).astype(F32)
-    gate_ref[...] = gate * (1.0 / (1.0 + jnp.exp(-gate)))
-
-
-def finish_body(me, in_ref, rate_ref, out_in_ref, elapsed_ref, map_ref, gate_ref, mixed_ref, carried):
+    out_ref[...] *= gate_token[...]
+
+
+def finish_body(me, in_ref, rate_ref, out_in_ref, share_ref, mixed_ref):
     states, channels = rate_ref.shape
-    tokens = elapsed_ref.shape[0]
     rate = rate_ref[...] * (-LOG2E)
     state = jnp.zeros((states, channels), F32)
     parts = channels // (in_ref.shape[2] - channels)
     for peer in range(in_ref.shape[0]):
         message = in_ref[peer].astype(F32)
-        final = message[:, :channels]
         ends = message[:parts, channels:] + message[parts : 2 * parts, channels:]
         length = jnp.concatenate([ends[part : part + 1] for part in range(parts)], axis=1)
-        state = jnp.where(peer < me[0], jnp.exp2(length * rate) * state + final, state)
-    corrected = []
-    for block in range(tokens // 8):
-        for inner in range(8):
-            t = block * 8 + inner
-            value = jnp.exp2(elapsed_ref[t : t + 1, :] * rate) * state
-            carried[inner * states : (inner + 1) * states, :] = value.astype(BF16)
-        corrected.append(
-            out_in_ref[block * 8 : block * 8 + 8, :]
-            + dot(map_ref[block * 8 : block * 8 + 8, :], carried[...])
-        )
-    scanned = jnp.transpose(jnp.concatenate(corrected, axis=0))
-    mixed_ref[...] = (scanned * gate_ref[...]).astype(BF16)
+        before = peer < me[0]
+        through = jnp.where(before, jnp.exp2(length * rate), 1.0)
+        final = jnp.where(before, message[:, :channels], 0.0)
+        state = through * state + final
+    scanned = out_in_ref[...]
+    for index in range(states):
+        scanned = scanned + share_ref[index].astype(F32) * state[index : index + 1, :]
+    mixed_ref[...] = jnp.transpose(scanned).astype(BF16)
 
 
 def local(
@@ -327,12 +344,13 @@
     weight = jnp.transpose(in_weight, (1, 2, 0)).reshape(2 * channels, width)
     pieces, starts = call(
         functools.partial(pack_body, slots),
-        (shape((peers * 16, features), BF16), shape((1, row_count), jnp.int32)),
+        (shape((peers, 16, row_count), BF16), shape((1, row_count), jnp.int32)),
         [SMEM, HBM, HBM, HBM],
         (me, in_hbm(group_target), in_hbm(tokens.T), in_hbm(starts)),
         [
             pltpu.SMEM((slots,), jnp.int32),
             pltpu.VMEM((features, row_count), BF16),
+            pltpu.VMEM((peers, 16, row_count), F32),
             pltpu.SemaphoreType.DMA((3,)),
         ],
     )
@@ -358,12 +376,12 @@
             pltpu.SemaphoreType.DMA((8,)),
         ],
     )
-    arrived = lax.all_to_all(pieces.reshape(peers, 16, features), "dp", 0, 0, tiled=True)
+    arrived = lax.all_to_all(pieces, "dp", 0, 0, tiled=True)
     payload = call(
         place_body,
         shape((features + 32, row_count), BF16),
         [VMEM, VMEM],
-        (arrived.reshape(peers * 16, features), my_gain),
+        (arrived, my_gain),
     )
     gathered = lax.all_gather(payload, "chan", axis=0)
     low, act = call(
@@ -386,15 +404,16 @@
         [VMEM] * 6,
         (lows, act, dtw, rate, rows, starts),
     )
-    out, elapsed, own_maps, gate = call(
+    out, share = call(
         functools.partial(side_body, features),
-        (by_token, by_token, shape((row_count, row_count), BF16), shape((channels, row_count), F32)),
+        (by_token, shape((states, row_count, channels), BF16)),
         [VMEM, HBM] + [VMEM] * 6,
         (gathered, weight, act, rate, rows, decay_step, drive_step, maps),
         [
             pltpu.VMEM((width, row_count), BF16),
             pltpu.VMEM((channels, width), BF16),
             pltpu.VMEM((8 * states, channels), BF16),
+            pltpu.VMEM((row_count, channels), F32),
             pltpu.SemaphoreType.DMA,
         ],
     )
@@ -402,9 +421,8 @@
     mixed = call(
         finish_body,
         shape((channels, row_count), BF16),
-        [SMEM] + [VMEM] * 6,
-        (me, ends, rate, out, elapsed, own_maps, gate),
-        [pltpu.VMEM((8 * states, channels), BF16)],
+        [SMEM] + [VMEM] * 4,
+        (me, ends, rate, out, share),
     )
     return mixed.T
 

time: 89.7 us -> 87.8 us (0.979)
  waiting for transfers between devices: 20.3 us -> 18.1 us
    all_to_all x1, waiting for transfers between devices: 8.82 us -> 6.97 us  [local(): arrived = lax.all_to_all(pieces, 'dp', 0, 0, tiled=True)]
  transfers between devices with their start and end apart: 2 -> 2, of which waited for: 2 -> 2; matrix products, arithmetic and copies ran while one was open for 1% -> 1% of each run, Pallas kernels for 5% -> 6%
where the time goes in v3:
time: 87.8 us; the launch traced here: 87.4 us
  blocking collectives  38.7 us (44%)
  waiting for transfers between devices  18.1 us (21%)
  starting transfers between devices  17.6 us (20%)
  Pallas kernels  12 us (14%)
    all_gather x1, blocking collectives, local(): gathered = lax.all_gather(payload, 'chan', axis=0)  21.6 us
    all_gather x1, blocking collectives, local(): lows = lax.all_gather(low, 'chan', axis=0)  17.1 us
    all_to_all x1, starting transfers between devices, local(): arrived = lax.all_to_all(pieces, 'dp', 0, 0, tiled=True)  13.7 us
    pallas_call x7, Pallas kernels, call(): pl.pallas_call(body, out_shape=outs, in_specs=specs, out_specs=jax.tree.m...  12 us
    all_to_all x1, waiting for transfers between devices, local(): ends = lax.all_to_all(send, 'dp', 0, 0, tiled=True)  11.2 us
    all_to_all x1, waiting for transfers between devices, local(): arrived = lax.all_to_all(pieces, 'dp', 0, 0, tiled=True)  6.97 us
    all_to_all x1, starting transfers between devices, local(): ends = lax.all_to_all(send, 'dp', 0, 0, tiled=True)  3.88 us
  transfers between devices with their start and end apart: 2, of which 2 were waited for; matrix products, arithmetic and copies ran while one was open for 1% of the time, Pallas kernels for 6%

profile of v3, /device:TPU:1, one launch (start us, length us, event | category | flops | bytes accessed | tf_op | source)
XLA Modules:
  0.0 87.4 jit_solution(5739211321216428306)
XLA Ops:
  0.0 2.0 %shard_map.118 = (bf16[32,16,128]{2,1,0:T(8,128)(2,1)}, s32[1,128]{1,0:T(1,128)S(1)}) custom-call(s32[1]{0:T(128)} %bitcast.me, s32[16]{0:T(128)} %target_hbm.1, bf16[160,128]{1,0:T(8,128)(2,1)} %bitcast.17, s32[1,128]{1,0:T(1,128)} %bitcast.19), custom_call_target="tpu_custom_call" | custom-call | tf_op jit(solution)/shard_map/pallas_call | solution.py:39
  2.1 13.7 %all-to-all-start = ((bf16[32,16,128]{2,1,0:T(8,128)(2,1)}), bf16[32,16,128]{2,1,0:T(8,128)(2,1)S(1)}, u32[]{:S(2)}, u32[]{:S(2)}) async-start(bf16[32,16,128]{2,1,0:T(8,128)(2,1)} %get-tuple-element.21), calls=%async_computation | async-start | bytes 262144 | tf_op jit(solution)/shard_map/all_to_all | solution.py:379
  15.8 0.8 dynamic_slice.3
  16.6 1.6 %shard_map.120 = (bf16[320,2560]{1,0:T(8,128)(2,1)S(1)}, bf16[192,320]{1,0:T(8,128)(2,1)S(1)}, bf16[160,320]{1,0:T(8,128)(2,1)S(1)}, f32[16,320]{1,0:T(8,128)S(1...) custom-call(bf16[640,2560]{1,0:T(8,128)(2,1)} %bitcast.14, bf16[192,320]{1,0:T(8,128)(2,1)} %bitcast.16, ...), custom_call_target="tpu_custom_call" | custom-call | tf_op jit(solution)/shard_map/pallas_call | solution.py:39
  18.2 0.0 copy-start
  18.2 7.0 %all-to-all-done.in_ref = bf16[32,16,128]{2,1,0:T(8,128)(2,1)S(1)} async-done(((bf16[32,16,128]{2,1,0:T(8,128)(2,1)}), bf16[32,16,128]{2,1,0:T(8,128)(2,1)S(1)}, u32[]{:S(2)}, u32[]{:S(2)}) %all-to-all-start) | async-done | bytes 131104 | tf_op jit(solution)/shard_map/all_to_all | solution.py:379
  25.1 0.1 broadcast_in_dim.2.gain_ref
  25.2 0.7 shard_map.119
  26.0 21.6 %all-gather = bf16[3072,128]{1,0:T(8,128)(2,1)S(1)} all-gather(bf16[192,128]{1,0:T(8,128)(2,1)S(1)} %shard_map.119), channel_id=2, replica_groups=mesh['dp'=32,'chan'=16] {'chan'}, dimensions={0}, use_global_device_ids=true | all-gather | bytes 835584 | tf_op jit(solution)/shard_map/all_gather | solution.py:386
  47.6 0.0 copy-done
  47.6 0.0 copy-start.1
  47.6 1.0 %shard_map.121 = (bf16[192,128]{1,0:T(8,128)(2,1)S(1)}, bf16[320,128]{1,0:T(8,128)(2,1)S(1)}) custom-call(bf16[16,192,128]{2,1,0:T(8,128)(2,1)S(1)} %bitcast.11, bf16[320,2560]{1,0:T(8,128)(2,1)S(1)} %get-tuple-element.22.weight_ref, f32[320,8]{1,0:T(8,128)S(1)} %get-tuple-element.23.taps_ref, bf16[192,320]{1,0:T(8,128)(2,1)S(1)} %get-tuple-element.24.proj_ref, ...), custom_call_target="tpu_custom_call" | custom-call | tf_op jit(solution)/shard_map/pallas_call | solution.py:39
  48.6 17.1 %all-gather.1 = bf16[3072,128]{1,0:T(8,128)(2,1)S(1)} all-gather(bf16[192,128]{1,0:T(8,128)(2,1)S(1)} %get-tuple-element.26), channel_id=3, replica_groups=mesh['dp'=32,'chan'=16] {'chan'}, dimensions={0}, use_global_device_ids=true | all-gather | bytes 835584 | tf_op jit(solution)/shard_map/all_gather | solution.py:394
  65.7 0.0 copy-done.1
  65.7 2.0 %shard_map.122 = (bf16[32,16,384]{2,1,0:T(8,128)(2,1)}, f32[128,320]{1,0:T(8,128)S(1)}, f32[128,320]{1,0:T(8,128)S(1)}, f32[32,128]{1,0:T(8,128)S(1)}) custom-call(bf16[16,192,128]{2,1,0:T(8,128)(2,1)S(1)} %bitcast.13, bf16[320,128]{1,0:T(8,128)(2,1)S(1)} %get-tuple-element.27.act_ref, bf16[160,320]{1,0:T(8,128)(2,1)S(1)} %copy-done.1, ...), custom_call_target="tpu_custom_call" | custom-call | tf_op jit(solution)/shard_map/pallas_call | solution.py:39
  67.7 3.9 %all-to-all-start.1 = ((bf16[32,16,384]{2,1,0:T(8,128)(2,1)}), bf16[32,16,384]{2,1,0:T(8,128)(2,1)S(1)}, u32[]{:S(2)}, u32[]{:S(2)}) async-start(bf16[32,16,384]{2,1,0:T(8,128)(2,1)} %get-tuple-element.31), calls=%async_computation.1 | async-start | bytes 786432 | tf_op jit(solution)/shard_map/all_to_all | solution.py:420
  71.6 3.4 %shard_map.123 = (f32[128,320]{1,0:T(8,128)S(1)}, bf16[16,128,320]{2,1,0:T(8,128)(2,1)S(1)}) custom-call(bf16[16,192,128]{2,1,0:T(8,128)(2,1)S(1)} %bitcast.12, bf16[640,2560]{1,0:T(8,128)(2,1)} %bitcast.15, bf16[320,128]{1,0:T(8,128)(2,1)S(1)} %get-tuple-element.27.act_ref, f32[16,320]{1,0:T(8,128)S(1)} %get-tuple-element.29.rate_ref, ...), custom_call_target="tpu_custom_call" | custom-call | tf_op jit(solution)/shard_map/pallas_call | solution.py:39
  75.0 11.2 %all-to-all-done.1.in_ref = bf16[32,16,384]{2,1,0:T(8,128)(2,1)S(1)} async-done(((bf16[32,16,384]{2,1,0:T(8,128)(2,1)}), bf16[32,16,384]{2,1,0:T(8,128)(2,1)S(1)}, u32[]{:S(2)}, u32[]{:S(2)}) %all-to-all-start.1) | async-done | bytes 393248 | tf_op jit(solution)/shard_map/all_to_all | solution.py:420
  86.1 1.3 %shard_map.124 = bf16[320,128]{1,0:T(8,128)(2,1)} custom-call(s32[1]{0:T(128)} %bitcast.me, bf16[32,16,384]{2,1,0:T(8,128)(2,1)S(1)} %all-to-all-done.1.in_ref, f32[16,320]{1,0:T(8,128)S(1)} %get-tuple-element.29.rate_ref, f32[128,320]{1,0:T(8,128)S(1)} %get-tuple-element.35.out_in_ref, bf16[16,128,320]{2,1,0:T(8,128)(2,1)S(1)} %get-tuple-element.36.share_ref), custom_call_target="tpu_custom_call" | custom-call | tf_op jit(solution)/shard_map/pallas_call | solution.py:39
Async XLA Ops:
  2.1 23.1 %all-to-all-start = ((bf16[32,16,128]{2,1,0:T(8,128)(2,1)}), bf16[32,16,128]{2,1,0:T(8,128)(2,1)S(1)}, u32[]{:S(2)}, u32[]{:S(2)}) async-start(bf16[32,16,128]{2,1,0:T(8,128)(2,1)} %get-tuple-element.21), calls=%async_computation | async-start | bytes 262144 | tf_op jit(solution)/shard_map/all_to_all | solution.py:379
  18.2 29.5 %copy-start = (bf16[160,320]{1,0:T(8,128)(2,1)}, bf16[160,320]{1,0:T(8,128)(2,1)S(1)}, u32[]{:S(2)}) copy-start(bf16[160,320]{1,0:T(8,128)(2,1)S(1)} %get-tuple-element.28.dtw_ref) | copy-start | bytes 307204
  47.6 18.1 %copy-start.1 = (bf16[160,320]{1,0:T(8,128)(2,1)S(1)}, bf16[160,320]{1,0:T(8,128)(2,1)}, u32[]{:S(2)}) copy-start(bf16[160,320]{1,0:T(8,128)(2,1)} %copy-done) | copy-start | bytes 307204
  67.7 18.4 %all-to-all-start.1 = ((bf16[32,16,384]{2,1,0:T(8,128)(2,1)}), bf16[32,16,384]{2,1,0:T(8,128)(2,1)S(1)}, u32[]{:S(2)}, u32[]{:S(2)}) async-start(bf16[32,16,384]{2,1,0:T(8,128)(2,1)} %get-tuple-element.31), calls=%async_computation.1 | async-start | bytes 786432 | tf_op jit(solution)/shard_map/all_to_all | solution.py:420

commit v4 on v3

--- a/solution.py
+++ b/solution.py
@@ -221,6 +221,29 @@
     low_ref[...] = dot(proj_ref[...], act).astype(BF16)
 
 
+def join(state, length, lanes):
+    states, channels = state.shape
+    spare = lanes - channels
+    pieces = channels // spare
+    length_high = length.astype(BF16).astype(F32)
+    line = iota((states, spare), 0)
+    ends = jnp.zeros((states, spare), F32)
+    for piece in range(pieces):
+        high = length_high[:, piece * spare : piece * spare + spare]
+        rest = length[:, piece * spare : piece * spare + spare] - high
+        ends = jnp.where(line == piece, high, ends)
+        ends = jnp.where(line == piece + pieces, rest, ends)
+    return jnp.concatenate([state, ends], axis=1).astype(BF16)
+
+
+def part(message, channels):
+    message = message.astype(F32)
+    pieces = channels // (message.shape[1] - channels)
+    ends = message[:pieces, channels:] + message[pieces : 2 * pieces, channels:]
+    length = jnp.concatenate([ends[piece : piece + 1] for piece in range(pieces)], axis=1)
+    return message[:, :channels], length
+
+
 def state_body(
     rank, in_ref, act_ref, dtw_ref, rate_ref, rows_ref, starts_ref,
     send_ref, decay_step, drive_step, maps_ref,
@@ -245,23 +268,35 @@
     for t in range(tokens):
         decay = jnp.exp2(decay_step[t : t + 1, :] * rate)
         state = decay * state + drive_step[t : t + 1, :] * in_map[:, t : t + 1]
-    spare = send_ref.shape[2] - channels
-    parts = channels // spare
-    last_high = last.astype(BF16).astype(F32)
-    line = iota((states, spare), 0)
-    ends = jnp.zeros((states, spare), F32)
-    for part in range(parts):
-        high_part = last_high[:, part * spare : part * spare + spare]
-        rest_part = last[:, part * spare : part * spare + spare] - high_part
-        ends = jnp.where(line == part, high_part, ends)
-        ends = jnp.where(line == part + parts, rest_part, ends)
-    final = jnp.concatenate([state, ends], axis=1).astype(BF16)
+    message = join(state, last, send_ref.shape[2])
     for peer in range(send_ref.shape[0]):
-        send_ref[peer] = final
+        send_ref[peer] = message
+
+
+def row_body(me, in_ref, rate_ref, send_ref, before_ref, length_ref):
+    states, channels = rate_ref.shape
+    rate = rate_ref[...] * (-LOG2E)
+    whole = jnp.zeros((states, channels), F32)
+    before = whole
+    whole_length = jnp.zeros((1, channels), F32)
+    before_length = whole_length
+    for peer in range(in_ref.shape[0]):
+        final, length = part(in_ref[peer], channels)
+        earlier = peer < me[0]
+        through = jnp.exp2(length * rate)
+        whole = through * whole + final
+        before = jnp.where(earlier, whole, before)
+        whole_length = whole_length + length
+        before_length = jnp.where(earlier, whole_length, before_length)
+    message = join(whole, whole_length, send_ref.shape[2])
+    for peer in range(send_ref.shape[0]):
+        send_ref[peer] = message
+    before_ref[...] = before
+    length_ref[...] = jnp.broadcast_to(before_length, length_ref.shape)
 
 
 def side_body(
-    features, in_ref, weight_hbm, act_ref, rate_ref, rows_ref, decay_step, drive_step, maps_ref,
+    features, in_ref, weight_hbm, act_ref, rate_ref, rows_ref, decay_step, drive_step, maps_ref, row_ref,
     out_ref, share_ref, wide, gate_weight, hidden, gate_token, sem,
 ):
     count = in_ref.shape[0]
@@ -306,19 +341,16 @@
     out_ref[...] *= gate_token[...]
 
 
-def finish_body(me, in_ref, rate_ref, out_in_ref, share_ref, mixed_ref):
+def finish_body(me, in_ref, rate_ref, before_ref, length_ref, out_in_ref, share_ref, mixed_ref):
     states, channels = rate_ref.shape
     rate = rate_ref[...] * (-LOG2E)
     state = jnp.zeros((states, channels), F32)
-    parts = channels // (in_ref.shape[2] - channels)
     for peer in range(in_ref.shape[0]):
-        message = in_ref[peer].astype(F32)
-        ends = message[:parts, channels:] + message[parts : 2 * parts, channels:]
-        length = jnp.concatenate([ends[part : part + 1] for part in range(parts)], axis=1)
-        before = peer < me[0]
-        through = jnp.where(before, jnp.exp2(length * rate), 1.0)
-        final = jnp.where(before, message[:, :channels], 0.0)
-        state = through * state + final
+        final, length = part(in_ref[peer], channels)
+        earlier = peer < me[0]
+        through = jnp.where(earlier, jnp.exp2(length * rate), 1.0)
+        state = through * state + jnp.where(earlier, final, 0.0)
+    state = jnp.exp2(length_ref[0:1, :] * rate) * state + before_ref[...]
     scanned = out_in_ref[...]
     for index in range(states):
         scanned = scanned + share_ref[index].astype(F32) * state[index : index + 1, :]
@@ -329,7 +361,8 @@
     tokens, norm_gain, in_weight, conv_weight, conv_bias, proj_weight, dt_weight, dt_bias,
     decay_rate, skip_gain, doc_starts, group_target,
 ):
-    peers = lax.axis_size("dp")
+    rows_of, in_row = lax.axis_size("z"), lax.axis_size("x")
+    peers = rows_of * in_row
     row_count, features = tokens.shape
     slots = group_target.shape[0]
     width = in_weight.shape[0]
@@ -337,7 +370,7 @@
     rank = dt_weight.shape[0]
     states = decay_rate.shape[1]
     shape = jax.ShapeDtypeStruct
-    me = lax.axis_index("dp").astype(jnp.int32).reshape(1)
+    me = lax.axis_index(("z", "x")).astype(jnp.int32).reshape(1)
     starts = doc_starts.reshape(1, row_count)
     my_gain = lax.dynamic_slice_in_dim(norm_gain, lax.axis_index("chan") * features, features)
     my_gain = jnp.broadcast_to(my_gain[:, None], (features, row_count))
@@ -376,7 +409,7 @@
             pltpu.SemaphoreType.DMA((8,)),
         ],
     )
-    arrived = lax.all_to_all(pieces, "dp", 0, 0, tiled=True)
+    arrived = lax.all_to_all(pieces, ("z", "x"), 0, 0, tiled=True)
     payload = call(
         place_body,
         shape((features + 32, row_count), BF16),
@@ -392,11 +425,12 @@
         [pltpu.VMEM((width, 2 * row_count), BF16)],
     )
     lows = lax.all_gather(low, "chan", axis=0)
+    lanes = -(-channels // 128) * 128
     by_token = shape((row_count, channels), F32)
     send, decay_step, drive_step, maps = call(
         functools.partial(state_body, rank),
         (
-            shape((peers, states, -(-channels // 128) * 128), BF16),
+            shape((in_row, states, lanes), BF16),
             by_token,
             by_token,
             shape((2 * states, row_count), F32),
@@ -404,11 +438,22 @@
         [VMEM] * 6,
         (lows, act, dtw, rate, rows, starts),
     )
+    in_row_ends = lax.all_to_all(send, "x", 0, 0, tiled=True)
+    send, before, before_length = call(
+        row_body,
+        (
+            shape((rows_of, states, lanes), BF16),
+            shape((states, channels), F32),
+            shape((8, channels), F32),
+        ),
+        [SMEM, VMEM, VMEM],
+        (lax.axis_index("x").astype(jnp.int32).reshape(1), in_row_ends, rate),
+    )
     out, share = call(
         functools.partial(side_body, features),
         (by_token, shape((states, row_count, channels), BF16)),
-        [VMEM, HBM] + [VMEM] * 6,
-        (gathered, weight, act, rate, rows, decay_step, drive_step, maps),
+        [VMEM, HBM] + [VMEM] * 7,
+        (gathered, weight, act, rate, rows, decay_step, drive_step, maps, before_length),
         [
             pltpu.VMEM((width, row_count), BF16),
             pltpu.VMEM((channels, width), BF16),
@@ -417,22 +462,27 @@
             pltpu.SemaphoreType.DMA,
         ],
     )
-    ends = lax.all_to_all(send, "dp", 0, 0, tiled=True)
+    ends = lax.all_to_all(send, "z", 0, 0, tiled=True)
+    my_row = lax.axis_index("z").astype(jnp.int32).reshape(1)
     mixed = call(
         finish_body,
         shape((channels, row_count), BF16),
-        [SMEM] + [VMEM] * 4,
-        (me, ends, rate, out, share),
+        [SMEM] + [VMEM] * 6,
+        (my_row, ends, rate, before, before_length, out, share),
     )
     return mixed.T
 
 
 def solution(mesh):
+    peers, chans = mesh.devices.shape
+    in_row = 4 if peers % 4 == 0 else 1
+    grid = mesh.devices.reshape(peers // in_row, in_row, chans)
+    mesh = jax.sharding.Mesh(grid, ("z", "x", "chan"))
     return jax.shard_map(
         local,
         mesh=mesh,
         in_specs=(
-            P("dp", "chan"),
+            P(("z", "x"), "chan"),
             P(),
             P(None, None, "chan"),
             P(None, "chan"),
@@ -442,9 +492,9 @@
             P("chan"),
             P("chan", None),
             P("chan"),
-            P("dp"),
-            P("dp"),
+            P(("z", "x")),
+            P(("z", "x")),
         ),
-        out_specs=P("dp", "chan"),
+        out_specs=P(("z", "x"), "chan"),
         check_vma=False,
     )

time: 87.8 us -> 88 us (level)
  waiting for transfers between devices: 18.1 us -> 11.1 us
  blocking collectives: 38.7 us -> 45.5 us
    all_to_all x2, waiting for transfers between devices: 18.1 us -> 11.1 us  [the longest x1 6.98 us: local(): arrived = lax.all_to_all(pieces, ('z', 'x'), 0, 0, tiled=True)]
    all_to_all x0 -> x1, blocking collectives: none -> 6.74 us  [local(): in_row_ends = lax.all_to_all(send, 'x', 0, 0, tiled=True)]
    pallas_call x7 -> x8, Pallas kernels: 12 us -> 12.2 us  [call(): pl.pallas_call(body, out_shape=outs, in_specs=specs, out_specs=jax.tree.m...]
where the time goes in v4:
time: 88 us; the launch traced here: 86.8 us
  blocking collectives  45.5 us (52%)
  starting transfers between devices  17.1 us (19%)
  Pallas kernels  12.2 us (14%)
  waiting for transfers between devices  11.1 us (13%)
    all_gather x1, blocking collectives, local(): gathered = lax.all_gather(payload, 'chan', axis=0)  21.6 us
    all_gather x1, blocking collectives, local(): lows = lax.all_gather(low, 'chan', axis=0)  17.1 us
    all_to_all x1, starting transfers between devices, local(): arrived = lax.all_to_all(pieces, ('z', 'x'), 0, 0, tiled=True)  13.7 us
    pallas_call x8, Pallas kernels, call(): pl.pallas_call(body, out_shape=outs, in_specs=specs, out_specs=jax.tree.m...  12.2 us
    all_to_all x1, waiting for transfers between devices, local(): arrived = lax.all_to_all(pieces, ('z', 'x'), 0, 0, tiled=True)  6.98 us
    all_to_all x1, blocking collectives, local(): in_row_ends = lax.all_to_all(send, 'x', 0, 0, tiled=True)  6.74 us
    all_to_all x1, waiting for transfers between devices, local(): ends = lax.all_to_all(send, 'z', 0, 0, tiled=True)  4.12 us
    all_to_all x1, starting transfers between devices, local(): ends = lax.all_to_all(send, 'z', 0, 0, tiled=True)  3.36 us
  transfers between devices with their start and end apart: 2, of which 2 were waited for; matrix products, arithmetic and copies ran while one was open for 1% of the time, Pallas kernels for 6%

profile of v4, /device:TPU:1, one launch (start us, length us, event | category | flops | bytes accessed | tf_op | source)
XLA Modules:
  0.0 86.8 jit_solution(15661104890867310323)
XLA Ops:
  0.0 2.0 %shard_map.118 = (bf16[32,16,128]{2,1,0:T(8,128)(2,1)}, s32[1,128]{1,0:T(1,128)S(1)}) custom-call(s32[1]{0:T(128)} %bitcast.2.me, s32[16]{0:T(128)} %target_hbm.1, bf16[160,128]{1,0:T(8,128)(2,1)} %bitcast.19, s32[1,128]{1,0:T(1,128)} %bitcast.21), custom_call_target="tpu_custom_call" | custom-call | tf_op jit(solution)/shard_map/pallas_call | solution.py:39
  2.1 13.7 %all-to-all-start = ((bf16[32,16,128]{2,1,0:T(8,128)(2,1)}), bf16[32,16,128]{2,1,0:T(8,128)(2,1)S(1)}, u32[]{:S(2)}, u32[]{:S(2)}) async-start(bf16[32,16,128]{2,1,0:T(8,128)(2,1)} %get-tuple-element.24), calls=%async_computation | async-start | bytes 262144 | tf_op jit(solution)/shard_map/all_to_all | solution.py:412
  15.8 0.8 dynamic_slice.3
  16.6 1.6 %shard_map.120 = (bf16[320,2560]{1,0:T(8,128)(2,1)S(1)}, bf16[192,320]{1,0:T(8,128)(2,1)S(1)}, bf16[160,320]{1,0:T(8,128)(2,1)S(1)}, f32[16,320]{1,0:T(8,128)S(1...) custom-call(bf16[640,2560]{1,0:T(8,128)(2,1)} %bitcast.16, bf16[192,320]{1,0:T(8,128)(2,1)} %bitcast.18, ...), custom_call_target="tpu_custom_call" | custom-call | tf_op jit(solution)/shard_map/pallas_call | solution.py:39
  18.2 7.0 %all-to-all-done.in_ref = bf16[32,16,128]{2,1,0:T(8,128)(2,1)S(1)} async-done(((bf16[32,16,128]{2,1,0:T(8,128)(2,1)}), bf16[32,16,128]{2,1,0:T(8,128)(2,1)S(1)}, u32[]{:S(2)}, u32[]{:S(2)}) %all-to-all-start) | async-done | bytes 131104 | tf_op jit(solution)/shard_map/all_to_all | solution.py:412
  25.1 0.1 broadcast_in_dim.2.gain_ref
  25.2 0.7 shard_map.119
  26.0 21.6 %all-gather = bf16[3072,128]{1,0:T(8,128)(2,1)S(1)} all-gather(bf16[192,128]{1,0:T(8,128)(2,1)S(1)} %shard_map.119), channel_id=2, replica_groups=mesh['z'=8,'x'=4,'chan'=16] {'chan'}, dimensions={0}, use_global_device_ids=true | all-gather | bytes 835584 | tf_op jit(solution)/shard_map/all_gather | solution.py:419
  47.6 1.0 %shard_map.121 = (bf16[192,128]{1,0:T(8,128)(2,1)S(1)}, bf16[320,128]{1,0:T(8,128)(2,1)S(1)}) custom-call(bf16[16,192,128]{2,1,0:T(8,128)(2,1)S(1)} %bitcast.13, bf16[320,2560]{1,0:T(8,128)(2,1)S(1)} %get-tuple-element.25.weight_ref, f32[320,8]{1,0:T(8,128)S(1)} %get-tuple-element.26.taps_ref, bf16[192,320]{1,0:T(8,128)(2,1)S(1)} %get-tuple-element.27.proj_ref, ...), custom_call_target="tpu_custom_call" | custom-call | tf_op jit(solution)/shard_map/pallas_call | solution.py:39
  48.6 17.1 %all-gather.1 = bf16[3072,128]{1,0:T(8,128)(2,1)S(1)} all-gather(bf16[192,128]{1,0:T(8,128)(2,1)S(1)} %get-tuple-element.29), channel_id=3, replica_groups=mesh['z'=8,'x'=4,'chan'=16] {'chan'}, dimensions={0}, use_global_device_ids=true | all-gather | bytes 835584 | tf_op jit(solution)/shard_map/all_gather | solution.py:427
  65.7 1.2 %shard_map.122 = (bf16[4,16,384]{2,1,0:T(8,128)(2,1)S(1)}, f32[128,320]{1,0:T(8,128)S(1)}, f32[128,320]{1,0:T(8,128)S(1)}, f32[32,128]{1,0:T(8,128)S(1)}) custom-call(bf16[16,192,128]{2,1,0:T(8,128)(2,1)S(1)} %bitcast.15, bf16[320,128]{1,0:T(8,128)(2,1)S(1)} %get-tuple-element.30.act_ref, bf16[160,320]{1,0:T(8,128)(2,1)S(1)} %get-tuple-element.31.dtw_ref, ...), custom_call_target="tpu_custom_call" | custom-call | tf_op jit(solution)/shard_map/pallas_call | solution.py:39
  67.0 6.7 %all_to_all.15.in_ref = bf16[4,16,384]{2,1,0:T(8,128)(2,1)S(1)} all-to-all(bf16[4,16,384]{2,1,0:T(8,128)(2,1)S(1)} %get-tuple-element.34), channel_id=1, replica_groups=mesh['z'=8,'x'=4,'chan'=16] {'x'}, dimensions={0} | all-to-all | bytes 98304 | tf_op jit(solution)/shard_map/all_to_all | solution.py:441
  73.7 1.1 %shard_map.123 = (bf16[8,16,384]{2,1,0:T(8,128)(2,1)}, f32[16,320]{1,0:T(8,128)S(1)}, f32[8,320]{1,0:T(8,128)S(1)}) custom-call(s32[1]{0:T(128)} %bitcast.1.me, bf16[4,16,384]{2,1,0:T(8,128)(2,1)S(1)} %all_to_all.15.in_ref, f32[16,320]{1,0:T(8,128)S(1)} %get-tuple-element.32.rate_ref), custom_call_target="tpu_custom_call" | custom-call | tf_op jit(solution)/shard_map/pallas_call | solution.py:39
  74.8 3.4 %all-to-all-start.2 = ((bf16[8,16,384]{2,1,0:T(8,128)(2,1)}), bf16[8,16,384]{2,1,0:T(8,128)(2,1)S(1)}, u32[]{:S(2)}, u32[]{:S(2)}) async-start(bf16[8,16,384]{2,1,0:T(8,128)(2,1)} %get-tuple-element.35), calls=%async_computation.2 | async-start | bytes 196608 | tf_op jit(solution)/shard_map/all_to_all | solution.py:465
  78.1 3.4 %shard_map.124 = (f32[128,320]{1,0:T(8,128)S(1)}, bf16[16,128,320]{2,1,0:T(8,128)(2,1)S(1)}) custom-call(bf16[16,192,128]{2,1,0:T(8,128)(2,1)S(1)} %bitcast.14, bf16[640,2560]{1,0:T(8,128)(2,1)} %bitcast.17, bf16[320,128]{1,0:T(8,128)(2,1)S(1)} %get-tuple-element.30.act_ref, f32[16,320]{1,0:T(8,128)S(1)} %get-tuple-element.32.rate_ref, ...), custom_call_target="tpu_custom_call" | custom-call | tf_op jit(solution)/shard_map/pallas_call | solution.py:39
  81.5 4.1 %all-to-all-done.2.in_ref = bf16[8,16,384]{2,1,0:T(8,128)(2,1)S(1)} async-done(((bf16[8,16,384]{2,1,0:T(8,128)(2,1)}), bf16[8,16,384]{2,1,0:T(8,128)(2,1)S(1)}, u32[]{:S(2)}, u32[]{:S(2)}) %all-to-all-start.2) | async-done | bytes 98336 | tf_op jit(solution)/shard_map/all_to_all | solution.py:465
  85.6 1.2 %shard_map.125 = bf16[320,128]{1,0:T(8,128)(2,1)} custom-call(s32[1]{0:T(128)} %bitcast.me, bf16[8,16,384]{2,1,0:T(8,128)(2,1)S(1)} %all-to-all-done.2.in_ref, f32[16,320]{1,0:T(8,128)S(1)} %get-tuple-element.32.rate_ref, f32[16,320]{1,0:T(8,128)S(1)} %get-tuple-element.36.before_ref, f32[8,320]{1,0:T(8,128)S(1)} %get-tuple-element.37.row_ref.length_ref, ...), custom_call_target="tpu_custom_call" | custom-call | tf_op jit(solution)/shard_map/pallas_call | solution.py:39
Async XLA Ops:
  2.1 23.1 %all-to-all-start = ((bf16[32,16,128]{2,1,0:T(8,128)(2,1)}), bf16[32,16,128]{2,1,0:T(8,128)(2,1)S(1)}, u32[]{:S(2)}, u32[]{:S(2)}) async-start(bf16[32,16,128]{2,1,0:T(8,128)(2,1)} %get-tuple-element.24), calls=%async_computation | async-start | bytes 262144 | tf_op jit(solution)/shard_map/all_to_all | solution.py:412
  74.8 10.9 %all-to-all-start.2 = ((bf16[8,16,384]{2,1,0:T(8,128)(2,1)}), bf16[8,16,384]{2,1,0:T(8,128)(2,1)S(1)}, u32[]{:S(2)}, u32[]{:S(2)}) async-start(bf16[8,16,384]{2,1,0:T(8,128)(2,1)} %get-tuple-element.35), calls=%async_computation.2 | async-start | bytes 196608 | tf_op jit(solution)/shard_map/all_to_all | solution.py:465

commit v5 on v4

--- a/solution.py
+++ b/solution.py
@@ -46,6 +46,26 @@
     )(*args)
 
 
+def swap_blocks(slabs):
+    lanes = 128
+    block = iota((16, lanes), 1) >> 3
+    slabs = list(slabs) + [None] * (16 - len(slabs))
+    for step in (8, 4, 2, 1):
+        keep = (block & step) == 0
+        for low in range(16):
+            if low & step:
+                continue
+            a, b = slabs[low], slabs[low | step]
+            if a is None and b is None:
+                continue
+            zero = jnp.zeros((16, lanes), F32)
+            up = zero if b is None else pltpu.roll(b, 8 * step, 1)
+            down = zero if a is None else pltpu.roll(a, lanes - 8 * step, 1)
+            slabs[low] = jnp.where(keep, zero if a is None else a, up)
+            slabs[low | step] = jnp.where(keep, down, zero if b is None else b)
+    return slabs
+
+
 def pack_body(slots, me, target_hbm, tok_hbm, starts_hbm, out_ref, starts_ref, target, tok_ref, pieces, sems):
     copies = [
         pltpu.make_async_copy(target_hbm, target, sems.at[0]),
@@ -55,7 +75,7 @@
     for copy in copies:
         copy.start()
     features, tokens = tok_ref.shape
-    peers = pieces.shape[0]
+    peers = out_ref.shape[0]
     parts = features // 16
     pieces[...] = jnp.zeros(pieces.shape, F32)
     lane = iota((16, tokens), 1)
@@ -66,15 +86,9 @@
         late & (place == features // 2 + 3 * (source >> 3) + (source & 7) - 5), 1.0, 0.0
     ).astype(BF16)
     copies[2].wait()
-    slabs = [tok_ref[16 * part : 16 * part + 16, :].astype(F32) for part in range(parts)]
-    groups = []
-    for group in range(slots):
-        piece = jnp.zeros((16, tokens), F32)
-        for part in range(parts):
-            shift = (8 * (part - group)) % tokens
-            moved = slabs[part] if shift == 0 else pltpu.roll(slabs[part], shift, 1)
-            piece = jnp.where((lane >> 3) == part, moved, piece)
-        groups.append(piece)
+    groups = swap_blocks(
+        [tok_ref[16 * piece : 16 * piece + 16, :].astype(F32) for piece in range(parts)]
+    )
     tails = dot(jnp.concatenate(groups, axis=0).astype(BF16), to_tail)
     copies[0].wait()
     copies[1].wait()
@@ -84,22 +98,22 @@
     flags = jnp.where(
         lane == 115, 1.0, jnp.where(lane == 114, one, jnp.where(lane == 113, one * two, 0.0))
     )
+    for group in range(slots):
+        where_to = target[group]
+        dev = lax.shift_right_logical(where_to, slots.bit_length() - 1)
+        slot = where_to & (slots - 1)
+        pieces[dev] = jnp.where(lane == 112, (slot + 1).astype(F32), groups[group])
+        follows = (slot == slots - 1) & (dev + 1 < peers)
+        pieces[jnp.where(follows, peers + dev + 1, 2 * peers)] = tails[16 * group : 16 * group + 16]
     after = me[0] + 1
-    pieces[jnp.minimum(after, peers - 1)] += jnp.where(after < peers, flags, 0.0)
-    for group in range(slots):
-        dev = target[group] // slots
-        slot = target[group] % slots
-        label = jnp.where(lane == 112, (slot + 1).astype(F32), 0.0)
-        pieces[dev] += groups[group] + label
-        follows = (slot == slots - 1) & (dev + 1 < peers)
-        tail = jnp.where(follows, tails[16 * group : 16 * group + 16], 0.0)
-        pieces[jnp.minimum(dev + 1, peers - 1)] += tail
-    out_ref[...] = pieces[...].astype(BF16)
+    for peer in range(peers):
+        whole = pieces[peer] + pieces[peers + peer] + jnp.where(after == peer, flags, 0.0)
+        out_ref[peer] = whole.astype(BF16)
 
 
 def fetch_body(
-    weight_hbm, proj_hbm, dtw_hbm, rate_hbm, taps_hbm, conv_bias_hbm, dt_bias_hbm, skip_hbm,
-    weight_ref, proj_ref, dtw_ref, rate_ref, cols_ref, rows_ref,
+    weight_hbm, proj_hbm, dtw_hbm, rate_hbm, taps_hbm, conv_bias_hbm, dt_bias_hbm, skip_hbm, starts_ref,
+    weight_ref, proj_ref, dtw_ref, rate_ref, cols_ref, rows_ref, first_ref,
     taps_in, conv_bias, dt_bias, skip, sems,
 ):
     taps, channels = taps_in.shape
@@ -124,6 +138,9 @@
     bias = conv_bias[...].reshape(1, channels)
     blank = jnp.zeros((8 - taps - 1, channels), F32)
     cols_ref[...] = jnp.transpose(jnp.concatenate([taps_in[...], bias, blank], axis=0))
+    tokens = starts_ref.shape[1]
+    first = jnp.transpose(jnp.broadcast_to(starts_ref[...].astype(F32), (tokens, tokens)))
+    first_ref[...] = jnp.broadcast_to(first[:, :1], first_ref.shape)
     rows_ref[0:1, :] = dt_bias[...].reshape(1, channels)
     rows_ref[1:2, :] = skip[...].reshape(1, channels)
     for copy in copies[4:]:
@@ -137,24 +154,19 @@
     slots = tokens // 8
     parts = features // 16
     arrived = in_ref[...].reshape(rows, tokens)
-    wide = arrived.astype(F32)
-    label = jnp.broadcast_to(wide[:, 112:113], (rows, 16 * slots))
-    key = (iota((rows, 16 * slots), 1) + 16 - (iota((rows, 16 * slots), 0) & 15)).astype(F32)
-    pick = jnp.where(label * 16.0 == key, 1.0, 0.0).astype(BF16)
-    ordered = dot(pick, arrived, TN)
-    total = jnp.sum(wide.reshape(peers, 16, tokens), axis=0)
+    spot = jnp.where(iota((16, tokens), 1) == 112, 1.0, 0.0).astype(BF16)
+    label = dot(spot, arrived, NT)[:1]
+    key = label * 16.0 + (iota((1, rows), 1) & 15).astype(F32)
+    want = (iota((16 * slots, rows), 0) + 16).astype(F32)
+    pick = jnp.where(key == want, 1.0, 0.0).astype(BF16)
+    ordered = dot(pick, arrived)
+    total = jnp.sum(in_ref[...].astype(F32), axis=0)
     lane = iota((16, tokens), 1)
     open_tail = jnp.where(lane >= tokens - 3, pltpu.roll(total, tokens - 3 - 113, 1), 0.0)
-    mains, tails = [], []
-    for part in range(parts):
-        slab = jnp.zeros((16, tokens), F32)
-        for slot in range(slots):
-            shift = (8 * (slot - part)) % tokens
-            piece = ordered[16 * slot : 16 * slot + 16]
-            moved = piece if shift == 0 else pltpu.roll(piece, shift, 1)
-            slab = jnp.where((lane >> 3) == slot, moved, slab)
-        mains.append(slab)
-        shift = (tokens - 3 - features // 2 - 3 * part) % tokens
+    mains = swap_blocks([ordered[16 * slot : 16 * slot + 16] for slot in range(slots)])[:parts]
+    tails = []
+    for piece in range(parts):
+        shift = (tokens - 3 - features // 2 - 3 * piece) % tokens
         tails.append((total if shift == 0 else pltpu.roll(total, shift, 1)) * open_tail)
     x_main = jnp.concatenate(mains, axis=0)
     x_tail = jnp.concatenate(tails, axis=0)
@@ -245,7 +257,7 @@
 
 
 def state_body(
-    rank, in_ref, act_ref, dtw_ref, rate_ref, rows_ref, starts_ref,
+    rank, in_ref, act_ref, dtw_ref, rate_ref, rows_ref, first_ref,
     send_ref, decay_step, drive_step, maps_ref,
 ):
     tokens = in_ref.shape[2]
@@ -257,10 +269,11 @@
     in_map = low[rank : rank + states]
     maps_ref[...] = low[rank:]
     raw = dot(dt_low, dtw_ref[...], TN) + rows_ref[0:1, :]
-    step = jnp.maximum(raw, 0.0) + jnp.log1p(jnp.exp(-jnp.abs(raw)))
+    small = jnp.exp(-jnp.abs(raw))
+    series = small * (1.0 - small * (0.5 - small * (1.0 / 3.0 - small * 0.25)))
+    step = jnp.maximum(raw, 0.0) + jnp.where(small < 0.01, series, jnp.log(1.0 + small))
     drive_step[...] = step * jnp.transpose(act_ref[...].astype(F32))
-    first = jnp.transpose(jnp.broadcast_to(starts_ref[...].astype(F32), (tokens, tokens)))
-    step = jnp.where(first[:, :1] > 0.5, FAR, step)
+    step = jnp.where(first_ref[...] > 0.5, FAR, step)
     decay_step[...] = step
     last = jnp.sum(step, axis=0, keepdims=True)
     rate = rate_ref[...] * (-LOG2E)
@@ -383,13 +396,13 @@
         [
             pltpu.SMEM((slots,), jnp.int32),
             pltpu.VMEM((features, row_count), BF16),
-            pltpu.VMEM((peers, 16, row_count), F32),
+            pltpu.VMEM((2 * peers + 1, 16, row_count), F32),
             pltpu.SemaphoreType.DMA((3,)),
         ],
     )
     weight = in_hbm(weight)
     sources = (proj_weight.T, dt_weight, decay_rate.T, conv_weight, conv_bias, dt_bias, skip_gain)
-    scan_weight, proj, dtw, rate, cols, rows = call(
+    scan_weight, proj, dtw, rate, cols, rows, first = call(
         fetch_body,
         (
             shape((channels, width), BF16),
@@ -398,9 +411,10 @@
             shape((states, channels), F32),
             shape((channels, 8), F32),
             shape((8, channels), F32),
+            shape((row_count, channels), F32),
         ),
-        [HBM] * 8,
-        (weight, *(in_hbm(source) for source in sources)),
+        [HBM] * 8 + [VMEM],
+        (weight, *(in_hbm(source) for source in sources), starts),
         [
             pltpu.VMEM(conv_weight.shape, F32),
             pltpu.VMEM((channels,), F32),
@@ -436,7 +450,7 @@
             shape((2 * states, row_count), F32),
         ),
         [VMEM] * 6,
-        (lows, act, dtw, rate, rows, starts),
+        (lows, act, dtw, rate, rows, first),
     )
     in_row_ends = lax.all_to_all(send, "x", 0, 0, tiled=True)
     send, before, before_length = call(

time: 88 us -> 87.9 us (level)
  no operation moved by 1% of the time
where the time goes in v5:
time: 87.9 us; the launch traced here: 86.7 us
  blocking collectives  45.5 us (52%)
  starting transfers between devices  17.1 us (19%)
  Pallas kernels  12.1 us (14%)
  waiting for transfers between devices  11.1 us (13%)
    all_gather x1, blocking collectives, local(): gathered = lax.all_gather(payload, 'chan', axis=0)  21.6 us
    all_gather x1, blocking collectives, local(): lows = lax.all_gather(low, 'chan', axis=0)  17.1 us
    all_to_all x1, starting transfers between devices, local(): arrived = lax.all_to_all(pieces, ('z', 'x'), 0, 0, tiled=True)  13.7 us
    pallas_call x8, Pallas kernels, call(): pl.pallas_call(body, out_shape=outs, in_specs=specs, out_specs=jax.tree.m...  12.1 us
    all_to_all x1, waiting for transfers between devices, local(): arrived = lax.all_to_all(pieces, ('z', 'x'), 0, 0, tiled=True)  6.98 us
    all_to_all x1, blocking collectives, local(): in_row_ends = lax.all_to_all(send, 'x', 0, 0, tiled=True)  6.74 us
    all_to_all x1, waiting for transfers between devices, local(): ends = lax.all_to_all(send, 'z', 0, 0, tiled=True)  4.12 us
    all_to_all x1, starting transfers between devices, local(): ends = lax.all_to_all(send, 'z', 0, 0, tiled=True)  3.36 us
  transfers between devices with their start and end apart: 2, of which 2 were waited for; matrix products, arithmetic and copies ran while one was open for 1% of the time, Pallas kernels for 6%

profile of v5, /device:TPU:1, one launch (start us, length us, event | category | flops | bytes accessed | tf_op | source)
XLA Modules:
  0.0 86.7 jit_solution(1269453281227628296)
XLA Ops:
  0.0 2.0 %shard_map.118 = (bf16[32,16,128]{2,1,0:T(8,128)(2,1)}, s32[1,128]{1,0:T(1,128)S(1)}) custom-call(s32[1]{0:T(128)} %bitcast.2.me, s32[16]{0:T(128)} %target_hbm.1, bf16[160,128]{1,0:T(8,128)(2,1)} %bitcast.19, s32[1,128]{1,0:T(1,128)} %bitcast.21), custom_call_target="tpu_custom_call" | custom-call | tf_op jit(solution)/shard_map/pallas_call | solution.py:39
  2.0 13.7 %all-to-all-start = ((bf16[32,16,128]{2,1,0:T(8,128)(2,1)}), bf16[32,16,128]{2,1,0:T(8,128)(2,1)S(1)}, u32[]{:S(2)}, u32[]{:S(2)}) async-start(bf16[32,16,128]{2,1,0:T(8,128)(2,1)} %get-tuple-element.25), calls=%async_computation | async-start | bytes 262144 | tf_op jit(solution)/shard_map/all_to_all | solution.py:426
  15.7 0.8 dynamic_slice.3
  16.5 1.6 %shard_map.120 = (bf16[320,2560]{1,0:T(8,128)(2,1)S(1)}, bf16[192,320]{1,0:T(8,128)(2,1)S(1)}, bf16[160,320]{1,0:T(8,128)(2,1)S(1)}, f32[16,320]{1,0:T(8,128)S(1...) custom-call(bf16[640,2560]{1,0:T(8,128)(2,1)} %bitcast.16, bf16[192,320]{1,0:T(8,128)(2,1)} %bitcast.18, ...), custom_call_target="tpu_custom_call" | custom-call | tf_op jit(solution)/shard_map/pallas_call | solution.py:39
  18.1 7.0 %all-to-all-done.in_ref = bf16[32,16,128]{2,1,0:T(8,128)(2,1)S(1)} async-done(((bf16[32,16,128]{2,1,0:T(8,128)(2,1)}), bf16[32,16,128]{2,1,0:T(8,128)(2,1)S(1)}, u32[]{:S(2)}, u32[]{:S(2)}) %all-to-all-start) | async-done | bytes 131104 | tf_op jit(solution)/shard_map/all_to_all | solution.py:426
  25.1 0.1 broadcast_in_dim.2.gain_ref
  25.2 0.7 shard_map.119
  25.9 21.6 %all-gather = bf16[3072,128]{1,0:T(8,128)(2,1)S(1)} all-gather(bf16[192,128]{1,0:T(8,128)(2,1)S(1)} %shard_map.119), channel_id=2, replica_groups=mesh['z'=8,'x'=4,'chan'=16] {'chan'}, dimensions={0}, use_global_device_ids=true | all-gather | bytes 835584 | tf_op jit(solution)/shard_map/all_gather | solution.py:433
  47.5 1.0 %shard_map.121 = (bf16[192,128]{1,0:T(8,128)(2,1)S(1)}, bf16[320,128]{1,0:T(8,128)(2,1)S(1)}) custom-call(bf16[16,192,128]{2,1,0:T(8,128)(2,1)S(1)} %bitcast.13, bf16[320,2560]{1,0:T(8,128)(2,1)S(1)} %get-tuple-element.27.weight_ref, f32[320,8]{1,0:T(8,128)S(1)} %get-tuple-element.28.taps_ref, bf16[192,320]{1,0:T(8,128)(2,1)S(1)} %get-tuple-element.29.proj_ref, ...), custom_call_target="tpu_custom_call" | custom-call | tf_op jit(solution)/shard_map/pallas_call | solution.py:39
  48.6 17.1 %all-gather.1 = bf16[3072,128]{1,0:T(8,128)(2,1)S(1)} all-gather(bf16[192,128]{1,0:T(8,128)(2,1)S(1)} %get-tuple-element.30), channel_id=3, replica_groups=mesh['z'=8,'x'=4,'chan'=16] {'chan'}, dimensions={0}, use_global_device_ids=true | all-gather | bytes 835584 | tf_op jit(solution)/shard_map/all_gather | solution.py:441
  65.6 1.2 %shard_map.122 = (bf16[4,16,384]{2,1,0:T(8,128)(2,1)S(1)}, f32[128,320]{1,0:T(8,128)S(1)}, f32[128,320]{1,0:T(8,128)S(1)}, f32[32,128]{1,0:T(8,128)S(1)}) custom-call(bf16[16,192,128]{2,1,0:T(8,128)(2,1)S(1)} %bitcast.15, bf16[320,128]{1,0:T(8,128)(2,1)S(1)} %get-tuple-element.31.act_ref, bf16[160,320]{1,0:T(8,128)(2,1)S(1)} %get-tuple-element.32.dtw_ref, ...), custom_call_target="tpu_custom_call" | custom-call | tf_op jit(solution)/shard_map/pallas_call | solution.py:39
  66.9 6.7 %all_to_all.15.in_ref = bf16[4,16,384]{2,1,0:T(8,128)(2,1)S(1)} all-to-all(bf16[4,16,384]{2,1,0:T(8,128)(2,1)S(1)} %get-tuple-element.36), channel_id=1, replica_groups=mesh['z'=8,'x'=4,'chan'=16] {'x'}, dimensions={0} | all-to-all | bytes 98304 | tf_op jit(solution)/shard_map/all_to_all | solution.py:455
  73.6 1.1 %shard_map.123 = (bf16[8,16,384]{2,1,0:T(8,128)(2,1)}, f32[16,320]{1,0:T(8,128)S(1)}, f32[8,320]{1,0:T(8,128)S(1)}) custom-call(s32[1]{0:T(128)} %bitcast.1.me, bf16[4,16,384]{2,1,0:T(8,128)(2,1)S(1)} %all_to_all.15.in_ref, f32[16,320]{1,0:T(8,128)S(1)} %get-tuple-element.33.rate_ref), custom_call_target="tpu_custom_call" | custom-call | tf_op jit(solution)/shard_map/pallas_call | solution.py:39
  74.7 3.4 %all-to-all-start.2 = ((bf16[8,16,384]{2,1,0:T(8,128)(2,1)}), bf16[8,16,384]{2,1,0:T(8,128)(2,1)S(1)}, u32[]{:S(2)}, u32[]{:S(2)}) async-start(bf16[8,16,384]{2,1,0:T(8,128)(2,1)} %get-tuple-element.37), calls=%async_computation.2 | async-start | bytes 196608 | tf_op jit(solution)/shard_map/all_to_all | solution.py:479
  78.1 3.4 %shard_map.124 = (f32[128,320]{1,0:T(8,128)S(1)}, bf16[16,128,320]{2,1,0:T(8,128)(2,1)S(1)}) custom-call(bf16[16,192,128]{2,1,0:T(8,128)(2,1)S(1)} %bitcast.14, bf16[640,2560]{1,0:T(8,128)(2,1)} %bitcast.17, bf16[320,128]{1,0:T(8,128)(2,1)S(1)} %get-tuple-element.31.act_ref, f32[16,320]{1,0:T(8,128)S(1)} %get-tuple-element.33.rate_ref, ...), custom_call_target="tpu_custom_call" | custom-call | tf_op jit(solution)/shard_map/pallas_call | solution.py:39
  81.4 4.1 %all-to-all-done.2.in_ref = bf16[8,16,384]{2,1,0:T(8,128)(2,1)S(1)} async-done(((bf16[8,16,384]{2,1,0:T(8,128)(2,1)}), bf16[8,16,384]{2,1,0:T(8,128)(2,1)S(1)}, u32[]{:S(2)}, u32[]{:S(2)}) %all-to-all-start.2) | async-done | bytes 98336 | tf_op jit(solution)/shard_map/all_to_all | solution.py:479
  85.5 1.2 %shard_map.125 = bf16[320,128]{1,0:T(8,128)(2,1)} custom-call(s32[1]{0:T(128)} %bitcast.me, bf16[8,16,384]{2,1,0:T(8,128)(2,1)S(1)} %all-to-all-done.2.in_ref, f32[16,320]{1,0:T(8,128)S(1)} %get-tuple-element.33.rate_ref, f32[16,320]{1,0:T(8,128)S(1)} %get-tuple-element.38.before_ref, f32[8,320]{1,0:T(8,128)S(1)} %get-tuple-element.39.row_ref.length_ref, ...), custom_call_target="tpu_custom_call" | custom-call | tf_op jit(solution)/shard_map/pallas_call | solution.py:39
Async XLA Ops:
  2.0 23.1 %all-to-all-start = ((bf16[32,16,128]{2,1,0:T(8,128)(2,1)}), bf16[32,16,128]{2,1,0:T(8,128)(2,1)S(1)}, u32[]{:S(2)}, u32[]{:S(2)}) async-start(bf16[32,16,128]{2,1,0:T(8,128)(2,1)} %get-tuple-element.25), calls=%async_computation | async-start | bytes 262144 | tf_op jit(solution)/shard_map/all_to_all | solution.py:426
  74.7 10.9 %all-to-all-start.2 = ((bf16[8,16,384]{2,1,0:T(8,128)(2,1)}), bf16[8,16,384]{2,1,0:T(8,128)(2,1)S(1)}, u32[]{:S(2)}, u32[]{:S(2)}) async-start(bf16[8,16,384]{2,1,0:T(8,128)(2,1)} %get-tuple-element.37), calls=%async_computation.2 | async-start | bytes 196608 | tf_op jit(solution)/shard_map/all_to_all | solution.py:479

commit v6 on v5

--- a/solution.py
+++ b/solution.py
@@ -286,7 +286,7 @@
         send_ref[peer] = message
 
 
-def row_body(me, in_ref, rate_ref, send_ref, before_ref, length_ref):
+def row_body(me, in_ref, rate_ref, out_ref, send_ref, before_ref, length_ref):
     states, channels = rate_ref.shape
     rate = rate_ref[...] * (-LOG2E)
     whole = jnp.zeros((states, channels), F32)
@@ -309,7 +309,7 @@
 
 
 def side_body(
-    features, in_ref, weight_hbm, act_ref, rate_ref, rows_ref, decay_step, drive_step, maps_ref, row_ref,
+    features, in_ref, weight_hbm, act_ref, rate_ref, rows_ref, decay_step, drive_step, maps_ref,
     out_ref, share_ref, wide, gate_weight, hidden, gate_token, sem,
 ):
     count = in_ref.shape[0]
@@ -453,6 +453,19 @@
         (lows, act, dtw, rate, rows, first),
     )
     in_row_ends = lax.all_to_all(send, "x", 0, 0, tiled=True)
+    out, share = call(
+        functools.partial(side_body, features),
+        (by_token, shape((states, row_count, channels), BF16)),
+        [VMEM, HBM] + [VMEM] * 6,
+        (gathered, weight, act, rate, rows, decay_step, drive_step, maps),
+        [
+            pltpu.VMEM((width, row_count), BF16),
+            pltpu.VMEM((channels, width), BF16),
+            pltpu.VMEM((8 * states, channels), BF16),
+            pltpu.VMEM((row_count, channels), F32),
+            pltpu.SemaphoreType.DMA,
+        ],
+    )
     send, before, before_length = call(
         row_body,
         (
@@ -460,21 +473,8 @@
             shape((states, channels), F32),
             shape((8, channels), F32),
         ),
-        [SMEM, VMEM, VMEM],
-        (lax.axis_index("x").astype(jnp.int32).reshape(1), in_row_ends, rate),
-    )
-    out, share = call(
-        functools.partial(side_body, features),
-        (by_token, shape((states, row_count, channels), BF16)),
-        [VMEM, HBM] + [VMEM] * 7,
-        (gathered, weight, act, rate, rows, decay_step, drive_step, maps, before_length),
-        [
-            pltpu.VMEM((width, row_count), BF16),
-            pltpu.VMEM((channels, width), BF16),
-            pltpu.VMEM((8 * states, channels), BF16),
-            pltpu.VMEM((row_count, channels), F32),
-            pltpu.SemaphoreType.DMA,
-        ],
+        [SMEM, VMEM, VMEM, VMEM],
+        (lax.axis_index("x").astype(jnp.int32).reshape(1), in_row_ends, rate, out),
     )
     ends = lax.all_to_all(send, "z", 0, 0, tiled=True)
     my_row = lax.axis_index("z").astype(jnp.int32).reshape(1)

time: 87.9 us -> 87.7 us (level)
  blocking collectives: 45.5 us -> 48.7 us
  waiting for transfers between devices: 11.1 us -> 7.98 us
    all_to_all x1, blocking collectives: 6.74 us -> 9.96 us  [local(): ends = lax.all_to_all(send, 'z', 0, 0, tiled=True)]
    all_to_all x1, waiting for transfers between devices: 4.12 us -> 1 us  [local(): in_row_ends = lax.all_to_all(send, 'x', 0, 0, tiled=True)]
where the time goes in v6:
time: 87.7 us; the launch traced here: 86.7 us
  blocking collectives  48.7 us (56%)
  starting transfers between devices  17 us (19%)
  Pallas kernels  12.1 us (14%)
  waiting for transfers between devices  7.98 us (9%)
    all_gather x1, blocking collectives, local(): gathered = lax.all_gather(payload, 'chan', axis=0)  21.6 us
    all_gather x1, blocking collectives, local(): lows = lax.all_gather(low, 'chan', axis=0)  17.1 us
    all_to_all x1, starting transfers between devices, local(): arrived = lax.all_to_all(pieces, ('z', 'x'), 0, 0, tiled=True)  13.7 us
    pallas_call x8, Pallas kernels, call(): pl.pallas_call(body, out_shape=outs, in_specs=specs, out_specs=jax.tree.m...  12.1 us
    all_to_all x1, blocking collectives, local(): ends = lax.all_to_all(send, 'z', 0, 0, tiled=True)  9.96 us
    all_to_all x1, waiting for transfers between devices, local(): arrived = lax.all_to_all(pieces, ('z', 'x'), 0, 0, tiled=True)  6.98 us
    all_to_all x1, starting transfers between devices, local(): in_row_ends = lax.all_to_all(send, 'x', 0, 0, tiled=True)  3.27 us
  transfers between devices with their start and end apart: 2, of which 2 were waited for; matrix products, arithmetic and copies ran while one was open for 1% of the time, Pallas kernels for 6%

profile of v6, /device:TPU:1, one launch (start us, length us, event | category | flops | bytes accessed | tf_op | source)
XLA Modules:
  0.0 86.7 jit_solution(11540467094350987905)
XLA Ops:
  0.0 2.0 %shard_map.118 = (bf16[32,16,128]{2,1,0:T(8,128)(2,1)}, s32[1,128]{1,0:T(1,128)S(1)}) custom-call(s32[1]{0:T(128)} %bitcast.2.me, s32[16]{0:T(128)} %target_hbm.1, bf16[160,128]{1,0:T(8,128)(2,1)} %bitcast.19, s32[1,128]{1,0:T(1,128)} %bitcast.21), custom_call_target="tpu_custom_call" | custom-call | tf_op jit(solution)/shard_map/pallas_call | solution.py:39
  2.0 13.7 %all-to-all-start = ((bf16[32,16,128]{2,1,0:T(8,128)(2,1)}), bf16[32,16,128]{2,1,0:T(8,128)(2,1)S(1)}, u32[]{:S(2)}, u32[]{:S(2)}) async-start(bf16[32,16,128]{2,1,0:T(8,128)(2,1)} %get-tuple-element.25), calls=%async_computation | async-start | bytes 262144 | tf_op jit(solution)/shard_map/all_to_all | solution.py:426
  15.7 0.8 dynamic_slice.3
  16.5 1.6 %shard_map.120 = (bf16[320,2560]{1,0:T(8,128)(2,1)S(1)}, bf16[192,320]{1,0:T(8,128)(2,1)S(1)}, bf16[160,320]{1,0:T(8,128)(2,1)S(1)}, f32[16,320]{1,0:T(8,128)S(1...) custom-call(bf16[640,2560]{1,0:T(8,128)(2,1)} %bitcast.16, bf16[192,320]{1,0:T(8,128)(2,1)} %bitcast.18, ...), custom_call_target="tpu_custom_call" | custom-call | tf_op jit(solution)/shard_map/pallas_call | solution.py:39
  18.1 7.0 %all-to-all-done.in_ref = bf16[32,16,128]{2,1,0:T(8,128)(2,1)S(1)} async-done(((bf16[32,16,128]{2,1,0:T(8,128)(2,1)}), bf16[32,16,128]{2,1,0:T(8,128)(2,1)S(1)}, u32[]{:S(2)}, u32[]{:S(2)}) %all-to-all-start) | async-done | bytes 131104 | tf_op jit(solution)/shard_map/all_to_all | solution.py:426
  25.1 0.1 broadcast_in_dim.2.gain_ref
  25.2 0.7 shard_map.119
  25.9 21.6 %all-gather = bf16[3072,128]{1,0:T(8,128)(2,1)S(1)} all-gather(bf16[192,128]{1,0:T(8,128)(2,1)S(1)} %shard_map.119), channel_id=2, replica_groups=mesh['z'=8,'x'=4,'chan'=16] {'chan'}, dimensions={0}, use_global_device_ids=true | all-gather | bytes 835584 | tf_op jit(solution)/shard_map/all_gather | solution.py:433
  47.5 1.0 %shard_map.121 = (bf16[192,128]{1,0:T(8,128)(2,1)S(1)}, bf16[320,128]{1,0:T(8,128)(2,1)S(1)}) custom-call(bf16[16,192,128]{2,1,0:T(8,128)(2,1)S(1)} %bitcast.13, bf16[320,2560]{1,0:T(8,128)(2,1)S(1)} %get-tuple-element.27.weight_ref, f32[320,8]{1,0:T(8,128)S(1)} %get-tuple-element.28.taps_ref, bf16[192,320]{1,0:T(8,128)(2,1)S(1)} %get-tuple-element.29.proj_ref, ...), custom_call_target="tpu_custom_call" | custom-call | tf_op jit(solution)/shard_map/pallas_call | solution.py:39
  48.6 17.1 %all-gather.1 = bf16[3072,128]{1,0:T(8,128)(2,1)S(1)} all-gather(bf16[192,128]{1,0:T(8,128)(2,1)S(1)} %get-tuple-element.30), channel_id=3, replica_groups=mesh['z'=8,'x'=4,'chan'=16] {'chan'}, dimensions={0}, use_global_device_ids=true | all-gather | bytes 835584 | tf_op jit(solution)/shard_map/all_gather | solution.py:441
  65.6 1.9 %shard_map.122 = (bf16[4,16,384]{2,1,0:T(8,128)(2,1)}, f32[128,320]{1,0:T(8,128)S(1)}, f32[128,320]{1,0:T(8,128)S(1)}, f32[32,128]{1,0:T(8,128)S(1)}) custom-call(bf16[16,192,128]{2,1,0:T(8,128)(2,1)S(1)} %bitcast.15, bf16[320,128]{1,0:T(8,128)(2,1)S(1)} %get-tuple-element.31.act_ref, bf16[160,320]{1,0:T(8,128)(2,1)S(1)} %get-tuple-element.32.dtw_ref, ...), custom_call_target="tpu_custom_call" | custom-call | tf_op jit(solution)/shard_map/pallas_call | solution.py:39
  67.5 3.3 %all-to-all-start.1 = ((bf16[4,16,384]{2,1,0:T(8,128)(2,1)}), bf16[4,16,384]{2,1,0:T(8,128)(2,1)S(1)}, u32[]{:S(2)}, u32[]{:S(2)}) async-start(bf16[4,16,384]{2,1,0:T(8,128)(2,1)} %get-tuple-element.36), calls=%async_computation.1 | async-start | bytes 98304 | tf_op jit(solution)/shard_map/all_to_all | solution.py:455
  70.8 3.3 %shard_map.123 = (f32[128,320]{1,0:T(8,128)S(1)}, bf16[16,128,320]{2,1,0:T(8,128)(2,1)S(1)}) custom-call(bf16[16,192,128]{2,1,0:T(8,128)(2,1)S(1)} %bitcast.14, bf16[640,2560]{1,0:T(8,128)(2,1)} %bitcast.17, bf16[320,128]{1,0:T(8,128)(2,1)S(1)} %get-tuple-element.31.act_ref, f32[16,320]{1,0:T(8,128)S(1)} %get-tuple-element.33.rate_ref, ...), custom_call_target="tpu_custom_call" | custom-call | tf_op jit(solution)/shard_map/pallas_call | solution.py:39
  74.2 1.0 %all-to-all-done.1.in_ref = bf16[4,16,384]{2,1,0:T(8,128)(2,1)S(1)} async-done(((bf16[4,16,384]{2,1,0:T(8,128)(2,1)}), bf16[4,16,384]{2,1,0:T(8,128)(2,1)S(1)}, u32[]{:S(2)}, u32[]{:S(2)}) %all-to-all-start.1) | async-done | bytes 49184 | tf_op jit(solution)/shard_map/all_to_all | solution.py:455
  75.2 0.4 shard_map.124
  75.6 10.0 %all_to_all.15.in_ref = bf16[8,16,384]{2,1,0:T(8,128)(2,1)S(1)} all-to-all(bf16[8,16,384]{2,1,0:T(8,128)(2,1)S(1)} %get-tuple-element.41), channel_id=1, replica_groups=mesh['z'=8,'x'=4,'chan'=16] {'z'}, dimensions={0} | all-to-all | bytes 196608 | tf_op jit(solution)/shard_map/all_to_all | solution.py:479
  85.6 1.1 %shard_map.125 = bf16[320,128]{1,0:T(8,128)(2,1)} custom-call(s32[1]{0:T(128)} %bitcast.me, bf16[8,16,384]{2,1,0:T(8,128)(2,1)S(1)} %all_to_all.15.in_ref, f32[16,320]{1,0:T(8,128)S(1)} %get-tuple-element.33.rate_ref, f32[16,320]{1,0:T(8,128)S(1)} %get-tuple-element.42.before_ref, f32[8,320]{1,0:T(8,128)S(1)} %get-tuple-element.43.length_ref, ...), custom_call_target="tpu_custom_call" | custom-call | tf_op jit(solution)/shard_map/pallas_call | solution.py:39
Async XLA Ops:
  2.0 23.1 %all-to-all-start = ((bf16[32,16,128]{2,1,0:T(8,128)(2,1)}), bf16[32,16,128]{2,1,0:T(8,128)(2,1)S(1)}, u32[]{:S(2)}, u32[]{:S(2)}) async-start(bf16[32,16,128]{2,1,0:T(8,128)(2,1)} %get-tuple-element.25), calls=%async_computation | async-start | bytes 262144 | tf_op jit(solution)/shard_map/all_to_all | solution.py:426
  67.5 7.6 %all-to-all-start.1 = ((bf16[4,16,384]{2,1,0:T(8,128)(2,1)}), bf16[4,16,384]{2,1,0:T(8,128)(2,1)S(1)}, u32[]{:S(2)}, u32[]{:S(2)}) async-start(bf16[4,16,384]{2,1,0:T(8,128)(2,1)} %get-tuple-element.36), calls=%async_computation.1 | async-start | bytes 98304 | tf_op jit(solution)/shard_map/all_to_all | solution.py:455

commit v7 on v5

--- a/solution.py
+++ b/solution.py
@@ -66,13 +66,34 @@
     return slabs
 
 
-def pack_body(slots, me, target_hbm, tok_hbm, starts_hbm, out_ref, starts_ref, target, tok_ref, pieces, sems):
+def pack_body(
+    slots, me, chan, target_hbm, tok_hbm, starts_hbm,
+    weight_hbm, proj_hbm, dtw_hbm, rate_hbm, taps_hbm, conv_bias_hbm, dt_bias_hbm, skip_hbm, gain_hbm,
+    out_ref, starts_ref, weight_ref, proj_ref, dtw_ref, rate_ref, cols_ref, rows_ref, first_ref, gain_ref,
+    target, tok_ref, pieces, taps_in, conv_bias, dt_bias, skip, gain, sems, more_sems,
+):
+    taps, channels = taps_in.shape
+    pairs = (
+        (taps_hbm, taps_in),
+        (conv_bias_hbm, conv_bias),
+        (dt_bias_hbm, dt_bias),
+        (skip_hbm, skip),
+        (gain_hbm, gain),
+        (weight_hbm.at[0:channels], weight_ref),
+        (proj_hbm, proj_ref),
+        (dtw_hbm, dtw_ref),
+        (rate_hbm, rate_ref),
+    )
+    fetches = [
+        pltpu.make_async_copy(source, into, more_sems.at[index])
+        for index, (source, into) in enumerate(pairs)
+    ]
     copies = [
         pltpu.make_async_copy(target_hbm, target, sems.at[0]),
         pltpu.make_async_copy(starts_hbm, starts_ref, sems.at[1]),
         pltpu.make_async_copy(tok_hbm, tok_ref, sems.at[2]),
     ]
-    for copy in copies:
+    for copy in copies + fetches:
         copy.start()
     features, tokens = tok_ref.shape
     peers = out_ref.shape[0]
@@ -109,42 +130,22 @@
     for peer in range(peers):
         whole = pieces[peer] + pieces[peers + peer] + jnp.where(after == peer, flags, 0.0)
         out_ref[peer] = whole.astype(BF16)
-
-
-def fetch_body(
-    weight_hbm, proj_hbm, dtw_hbm, rate_hbm, taps_hbm, conv_bias_hbm, dt_bias_hbm, skip_hbm, starts_ref,
-    weight_ref, proj_ref, dtw_ref, rate_ref, cols_ref, rows_ref, first_ref,
-    taps_in, conv_bias, dt_bias, skip, sems,
-):
-    taps, channels = taps_in.shape
-    pairs = (
-        (taps_hbm, taps_in),
-        (conv_bias_hbm, conv_bias),
-        (dt_bias_hbm, dt_bias),
-        (skip_hbm, skip),
-        (weight_hbm.at[0:channels], weight_ref),
-        (proj_hbm, proj_ref),
-        (dtw_hbm, dtw_ref),
-        (rate_hbm, rate_ref),
-    )
-    copies = [
-        pltpu.make_async_copy(source, target, sems.at[index])
-        for index, (source, target) in enumerate(pairs)
-    ]
-    for copy in copies:
-        copy.start()
-    for copy in copies[:4]:
-        copy.wait()
+    for fetch in fetches[:5]:
+        fetch.wait()
     bias = conv_bias[...].reshape(1, channels)
     blank = jnp.zeros((8 - taps - 1, channels), F32)
     cols_ref[...] = jnp.transpose(jnp.concatenate([taps_in[...], bias, blank], axis=0))
-    tokens = starts_ref.shape[1]
     first = jnp.transpose(jnp.broadcast_to(starts_ref[...].astype(F32), (tokens, tokens)))
     first_ref[...] = jnp.broadcast_to(first[:, :1], first_ref.shape)
     rows_ref[0:1, :] = dt_bias[...].reshape(1, channels)
     rows_ref[1:2, :] = skip[...].reshape(1, channels)
-    for copy in copies[4:]:
-        copy.wait()
+    gains = gain[...].reshape(1, gain.shape[0])
+    mine = jnp.zeros((1, features), F32)
+    for index in range(gain.shape[0] // features):
+        mine = jnp.where(chan[0] == index, gains[:, index * features : (index + 1) * features], mine)
+    gain_ref[...] = jnp.transpose(jnp.broadcast_to(mine, (tokens, features)))
+    for fetch in fetches[5:]:
+        fetch.wait()
 
 
 def place_body(in_ref, gain_ref, out_ref):
@@ -277,10 +278,18 @@
     decay_step[...] = step
     last = jnp.sum(step, axis=0, keepdims=True)
     rate = rate_ref[...] * (-LOG2E)
-    state = jnp.zeros((states, channels), F32)
-    for t in range(tokens):
-        decay = jnp.exp2(decay_step[t : t + 1, :] * rate)
-        state = decay * state + drive_step[t : t + 1, :] * in_map[:, t : t + 1]
+    stretches = 4
+    length = tokens // stretches
+    parts = [jnp.zeros((states, channels), F32)] * stretches
+    for offset in range(length):
+        for index in range(stretches):
+            t = index * length + offset
+            decay = jnp.exp2(decay_step[t : t + 1, :] * rate)
+            parts[index] = decay * parts[index] + drive_step[t : t + 1, :] * in_map[:, t : t + 1]
+    state = parts[0]
+    for index in range(1, stretches):
+        spent = jnp.sum(step[index * length : (index + 1) * length], axis=0, keepdims=True)
+        state = jnp.exp2(spent * rate) * state + parts[index]
     message = join(state, last, send_ref.shape[2])
     for peer in range(send_ref.shape[0]):
         send_ref[peer] = message
@@ -385,26 +394,17 @@
     shape = jax.ShapeDtypeStruct
     me = lax.axis_index(("z", "x")).astype(jnp.int32).reshape(1)
     starts = doc_starts.reshape(1, row_count)
-    my_gain = lax.dynamic_slice_in_dim(norm_gain, lax.axis_index("chan") * features, features)
-    my_gain = jnp.broadcast_to(my_gain[:, None], (features, row_count))
+    chan = lax.axis_index("chan").astype(jnp.int32).reshape(1)
     weight = jnp.transpose(in_weight, (1, 2, 0)).reshape(2 * channels, width)
-    pieces, starts = call(
+    weight = in_hbm(weight)
+    sources = (
+        proj_weight.T, dt_weight, decay_rate.T, conv_weight, conv_bias, dt_bias, skip_gain, norm_gain,
+    )
+    pieces, starts, scan_weight, proj, dtw, rate, cols, rows, first, my_gain = call(
         functools.partial(pack_body, slots),
-        (shape((peers, 16, row_count), BF16), shape((1, row_count), jnp.int32)),
-        [SMEM, HBM, HBM, HBM],
-        (me, in_hbm(group_target), in_hbm(tokens.T), in_hbm(starts)),
-        [
-            pltpu.SMEM((slots,), jnp.int32),
-            pltpu.VMEM((features, row_count), BF16),
-            pltpu.VMEM((2 * peers + 1, 16, row_count), F32),
-            pltpu.SemaphoreType.DMA((3,)),
-        ],
-    )
-    weight = in_hbm(weight)
-    sources = (proj_weight.T, dt_weight, decay_rate.T, conv_weight, conv_bias, dt_bias, skip_gain)
-    scan_weight, proj, dtw, rate, cols, rows, first = call(
-        fetch_body,
         (
+            shape((peers, 16, row_count), BF16),
+            shape((1, row_count), jnp.int32),
             shape((channels, width), BF16),
             shape((rank + 2 * states, channels), BF16),
             shape((rank, channels), BF16),
@@ -412,15 +412,24 @@
             shape((channels, 8), F32),
             shape((8, channels), F32),
             shape((row_count, channels), F32),
+            shape((features, row_count), F32),
         ),
-        [HBM] * 8 + [VMEM],
-        (weight, *(in_hbm(source) for source in sources), starts),
+        [SMEM, SMEM] + [HBM] * 12,
+        (
+            me, chan, in_hbm(group_target), in_hbm(tokens.T), in_hbm(starts), weight,
+            *(in_hbm(source) for source in sources),
+        ),
         [
+            pltpu.SMEM((slots,), jnp.int32),
+            pltpu.VMEM((features, row_count), BF16),
+            pltpu.VMEM((2 * peers + 1, 16, row_count), F32),
             pltpu.VMEM(conv_weight.shape, F32),
             pltpu.VMEM((channels,), F32),
             pltpu.VMEM((channels,), F32),
             pltpu.VMEM((channels,), F32),
-            pltpu.SemaphoreType.DMA((8,)),
+            pltpu.VMEM((width,), F32),
+            pltpu.SemaphoreType.DMA((3,)),
+            pltpu.SemaphoreType.DMA((9,)),
         ],
     )
     arrived = lax.all_to_all(pieces, ("z", "x"), 0, 0, tiled=True)

time: 87.9 us -> 88.2 us (level)
  blocking collectives: 45.5 us -> 68.3 us
  starting transfers between devices: 17.1 us -> 3.36 us
  waiting for transfers between devices: 11.1 us -> 4.12 us
  Pallas kernels: 12.1 us -> 11.2 us
    all_to_all x0 -> x1, blocking collectives: none -> 22.9 us  [local(): arrived = lax.all_to_all(pieces, ('z', 'x'), 0, 0, tiled=True)]
    all_to_all x1 -> x0, starting transfers between devices: 13.7 us -> none  [local(): arrived = lax.all_to_all(pieces, ('z', 'x'), 0, 0, tiled=True)]
    all_to_all x1 -> x0, waiting for transfers between devices: 6.98 us -> none  [local(): arrived = lax.all_to_all(pieces, ('z', 'x'), 0, 0, tiled=True)]
    pallas_call x8 -> x7, Pallas kernels: 12.1 us -> 11.2 us  [call(): pl.pallas_call(body, out_shape=outs, in_specs=specs, out_specs=jax.tree.m...]
  transfers between devices with their start and end apart: 2 -> 1, of which waited for: 2 -> 1; matrix products, arithmetic and copies ran while one was open for 1% -> 0% of each run, Pallas kernels for 6% -> 4%
where the time goes in v7:
time: 88.2 us; the launch traced here: 87.1 us
  blocking collectives  68.3 us (77%)
  Pallas kernels  11.2 us (13%)
  waiting for transfers between devices  4.12 us (5%)
  starting transfers between devices  3.36 us (4%)
    all_to_all x1, blocking collectives, local(): arrived = lax.all_to_all(pieces, ('z', 'x'), 0, 0, tiled=True)  22.9 us
    all_gather x1, blocking collectives, local(): gathered = lax.all_gather(payload, 'chan', axis=0)  21.6 us
    all_gather x1, blocking collectives, local(): lows = lax.all_gather(low, 'chan', axis=0)  17.1 us
    pallas_call x7, Pallas kernels, call(): pl.pallas_call(body, out_shape=outs, in_specs=specs, out_specs=jax.tree.m...  11.2 us
    all_to_all x1, blocking collectives, local(): in_row_ends = lax.all_to_all(send, 'x', 0, 0, tiled=True)  6.74 us
    all_to_all x1, waiting for transfers between devices, local(): ends = lax.all_to_all(send, 'z', 0, 0, tiled=True)  4.12 us
    all_to_all x1, starting transfers between devices, local(): ends = lax.all_to_all(send, 'z', 0, 0, tiled=True)  3.36 us
  transfers between devices with their start and end apart: 1, of which 1 were waited for; matrix products, arithmetic and copies ran while one was open for 0% of the time, Pallas kernels for 4%

profile of v7, /device:TPU:1, one launch (start us, length us, event | category | flops | bytes accessed | tf_op | source)
XLA Modules:
  0.0 87.1 jit_solution(2535595956308510695)
XLA Ops:
  0.0 2.7 %shard_map.118 = (bf16[32,16,128]{2,1,0:T(8,128)(2,1)S(1)}, s32[1,128]{1,0:T(1,128)S(1)}, bf16[320,2560]{1,0:T(8,128)(2,1)S(1)}, bf16[192,320]{1,0:T(8,128)(2,1)...) custom-call(s32[1]{0:T(128)} %bitcast.2.me, ...), custom_call_target="tpu_custom_call" | custom-call | tf_op jit(solution)/shard_map/pallas_call | solution.py:39
  2.7 22.9 %all_to_all.15.in_ref = bf16[32,16,128]{2,1,0:T(8,128)(2,1)S(1)} all-to-all(bf16[32,16,128]{2,1,0:T(8,128)(2,1)S(1)} %get-tuple-element.26), channel_id=1, replica_groups=mesh['z'=8,'x'=4,'chan'=16] {'z','x'}, dimensions={0} | all-to-all | bytes 262144 | tf_op jit(solution)/shard_map/all_to_all | solution.py:435
  25.5 0.7 shard_map.119
  26.3 21.6 %all-gather = bf16[3072,128]{1,0:T(8,128)(2,1)S(1)} all-gather(bf16[192,128]{1,0:T(8,128)(2,1)S(1)} %shard_map.119), channel_id=2, replica_groups=mesh['z'=8,'x'=4,'chan'=16] {'chan'}, dimensions={0}, use_global_device_ids=true | all-gather | bytes 835584 | tf_op jit(solution)/shard_map/all_gather | solution.py:442
  47.9 1.0 %shard_map.120 = (bf16[192,128]{1,0:T(8,128)(2,1)S(1)}, bf16[320,128]{1,0:T(8,128)(2,1)S(1)}) custom-call(bf16[16,192,128]{2,1,0:T(8,128)(2,1)S(1)} %bitcast.14, bf16[320,2560]{1,0:T(8,128)(2,1)S(1)} %get-tuple-element.28.weight_ref, f32[320,8]{1,0:T(8,128)S(1)} %get-tuple-element.29.taps_ref, bf16[192,320]{1,0:T(8,128)(2,1)S(1)} %get-tuple-element.30.proj_ref, ...), custom_call_target="tpu_custom_call" | custom-call | tf_op jit(solution)/shard_map/pallas_call | solution.py:39
  48.9 17.1 %all-gather.1 = bf16[3072,128]{1,0:T(8,128)(2,1)S(1)} all-gather(bf16[192,128]{1,0:T(8,128)(2,1)S(1)} %get-tuple-element.32), channel_id=3, replica_groups=mesh['z'=8,'x'=4,'chan'=16] {'chan'}, dimensions={0}, use_global_device_ids=true | all-gather | bytes 835584 | tf_op jit(solution)/shard_map/all_gather | solution.py:450
  66.0 1.2 %shard_map.121 = (bf16[4,16,384]{2,1,0:T(8,128)(2,1)S(1)}, f32[128,320]{1,0:T(8,128)S(1)}, f32[128,320]{1,0:T(8,128)S(1)}, f32[32,128]{1,0:T(8,128)S(1)}) custom-call(bf16[16,192,128]{2,1,0:T(8,128)(2,1)S(1)} %bitcast.16, bf16[320,128]{1,0:T(8,128)(2,1)S(1)} %get-tuple-element.33.act_ref, bf16[160,320]{1,0:T(8,128)(2,1)S(1)} %get-tuple-element.34.dtw_ref, ...), custom_call_target="tpu_custom_call" | custom-call | tf_op jit(solution)/shard_map/pallas_call | solution.py:39
  67.2 6.7 %all_to_all.16.in_ref = bf16[4,16,384]{2,1,0:T(8,128)(2,1)S(1)} all-to-all(bf16[4,16,384]{2,1,0:T(8,128)(2,1)S(1)} %get-tuple-element.38), channel_id=1, replica_groups=mesh['z'=8,'x'=4,'chan'=16] {'x'}, dimensions={0} | all-to-all | bytes 98304 | tf_op jit(solution)/shard_map/all_to_all | solution.py:464
  74.0 1.1 %shard_map.122 = (bf16[8,16,384]{2,1,0:T(8,128)(2,1)}, f32[16,320]{1,0:T(8,128)S(1)}, f32[8,320]{1,0:T(8,128)S(1)}) custom-call(s32[1]{0:T(128)} %bitcast.1.me, bf16[4,16,384]{2,1,0:T(8,128)(2,1)S(1)} %all_to_all.16.in_ref, f32[16,320]{1,0:T(8,128)S(1)} %get-tuple-element.35.rate_ref), custom_call_target="tpu_custom_call" | custom-call | tf_op jit(solution)/shard_map/pallas_call | solution.py:39
  75.1 3.4 %all-to-all-start.2 = ((bf16[8,16,384]{2,1,0:T(8,128)(2,1)}), bf16[8,16,384]{2,1,0:T(8,128)(2,1)S(1)}, u32[]{:S(2)}, u32[]{:S(2)}) async-start(bf16[8,16,384]{2,1,0:T(8,128)(2,1)} %get-tuple-element.39), calls=%async_computation.2 | async-start | bytes 196608 | tf_op jit(solution)/shard_map/all_to_all | solution.py:488
  78.4 3.4 %shard_map.123 = (f32[128,320]{1,0:T(8,128)S(1)}, bf16[16,128,320]{2,1,0:T(8,128)(2,1)S(1)}) custom-call(bf16[16,192,128]{2,1,0:T(8,128)(2,1)S(1)} %bitcast.15, bf16[640,2560]{1,0:T(8,128)(2,1)} %bitcast.18, bf16[320,128]{1,0:T(8,128)(2,1)S(1)} %get-tuple-element.33.act_ref, f32[16,320]{1,0:T(8,128)S(1)} %get-tuple-element.35.rate_ref, ...), custom_call_target="tpu_custom_call" | custom-call | tf_op jit(solution)/shard_map/pallas_call | solution.py:39
  81.8 4.1 %all-to-all-done.2.in_ref = bf16[8,16,384]{2,1,0:T(8,128)(2,1)S(1)} async-done(((bf16[8,16,384]{2,1,0:T(8,128)(2,1)}), bf16[8,16,384]{2,1,0:T(8,128)(2,1)S(1)}, u32[]{:S(2)}, u32[]{:S(2)}) %all-to-all-start.2) | async-done | bytes 98336 | tf_op jit(solution)/shard_map/all_to_all | solution.py:488
  85.9 1.2 %shard_map.124 = bf16[320,128]{1,0:T(8,128)(2,1)} custom-call(s32[1]{0:T(128)} %bitcast.me, bf16[8,16,384]{2,1,0:T(8,128)(2,1)S(1)} %all-to-all-done.2.in_ref, f32[16,320]{1,0:T(8,128)S(1)} %get-tuple-element.35.rate_ref, f32[16,320]{1,0:T(8,128)S(1)} %get-tuple-element.40.before_ref, f32[8,320]{1,0:T(8,128)S(1)} %get-tuple-element.41.row_ref.length_ref, ...), custom_call_target="tpu_custom_call" | custom-call | tf_op jit(solution)/shard_map/pallas_call | solution.py:39
Async XLA Ops:
  75.1 10.9 %all-to-all-start.2 = ((bf16[8,16,384]{2,1,0:T(8,128)(2,1)}), bf16[8,16,384]{2,1,0:T(8,128)(2,1)S(1)}, u32[]{:S(2)}, u32[]{:S(2)}) async-start(bf16[8,16,384]{2,1,0:T(8,128)(2,1)} %get-tuple-element.39), calls=%async_computation.2 | async-start | bytes 196608 | tf_op jit(solution)/shard_map/all_to_all | solution.py:488

commit v8 on v5

--- a/solution.py
+++ b/solution.py
@@ -179,20 +179,31 @@
     for part in range(features // 16):
         shift = (8 * part - (tokens - 8)) % tokens
         packed = packed + pltpu.roll(x_tail[16 * part : 16 * part + 16], shift, 1)
-    out_ref[features : features + 16, :] = packed.astype(BF16)
+    line = iota((16, tokens), 0)
+    first_lane = features // 2
+    spare = (lane >= first_lane) & (lane < first_lane + 32)
     main_high = main_sq.astype(BF16).astype(F32)
     tail_high = tail_sq.astype(BF16).astype(F32)
-    line = iota((16, tokens), 0)
-    sums = jnp.where(
-        line == 0,
-        main_high,
-        jnp.where(
-            line == 1,
-            main_sq - main_high,
-            jnp.where(line == 2, tail_high, jnp.where(line == 3, tail_sq - tail_high, 0.0)),
-        ),
-    )
-    out_ref[features + 16 : features + 32, :] = sums.astype(BF16)
+    rows = [(main_high, part) for part in range(4)] + [(main_sq - main_high, part) for part in range(4)]
+    rows += [(tail_high, 3), (tail_sq - tail_high, 3)]
+    for index, (value, part) in enumerate(rows):
+        moved = pltpu.roll(jnp.broadcast_to(value, (16, tokens)), (first_lane - 32 * part) % tokens, 1)
+        packed = jnp.where(spare & (line == index), moved, packed)
+    out_ref[features : features + 16, :] = packed.astype(BF16)
+
+
+def square_sums(total, features):
+    tokens = total.shape[1]
+    first_lane = features // 2
+    lane = iota((8, tokens), 1)
+    main = jnp.zeros((8, tokens), F32)
+    for part in range(4):
+        row = jnp.broadcast_to(total[part : part + 1] + total[part + 4 : part + 5], (8, tokens))
+        moved = pltpu.roll(row, (32 * part - first_lane) % tokens, 1)
+        main = jnp.where((lane >> 5) == part, moved, main)
+    row = jnp.broadcast_to(total[8:9] + total[9:10], (8, tokens))
+    tail = pltpu.roll(row, (96 - first_lane) % tokens, 1)
+    return main[:1], jnp.where(lane >= 96, tail, 0.0)[:1]
 
 
 def project_body(
@@ -207,13 +218,14 @@
         base = peer * features
         wide[base : base + features, 0:tokens] = in_ref[peer, 0:features, :]
         packed = in_ref[peer, features : features + 16, :].astype(F32)
-        sums = sums + in_ref[peer, features + 16 : features + 32, :].astype(F32)
+        sums = sums + packed
         for part in range(features // 16):
             shift = (tokens - 8 - 8 * part) % tokens
             moved = packed if shift == 0 else pltpu.roll(packed, shift, 1)
             wide[base + 16 * part : base + 16 * part + 16, tokens:] = moved.astype(BF16)
-    scale_main = lax.rsqrt((sums[0:1] + sums[1:2]) / width + EPSILON)
-    scale_tail = lax.rsqrt((sums[2:3] + sums[3:4]) / width + EPSILON)
+    main_sq, tail_sq = square_sums(sums, features)
+    scale_main = lax.rsqrt(main_sq / width + EPSILON)
+    scale_tail = lax.rsqrt(tail_sq / width + EPSILON)
     both = dot(weight_ref[...], wide[...])
     x_in = (both[:, :tokens] * scale_main).astype(BF16).astype(F32)
     tail = (both[:, tokens:] * scale_tail).astype(BF16).astype(F32)
@@ -277,10 +289,18 @@
     decay_step[...] = step
     last = jnp.sum(step, axis=0, keepdims=True)
     rate = rate_ref[...] * (-LOG2E)
-    state = jnp.zeros((states, channels), F32)
-    for t in range(tokens):
-        decay = jnp.exp2(decay_step[t : t + 1, :] * rate)
-        state = decay * state + drive_step[t : t + 1, :] * in_map[:, t : t + 1]
+    stretches = 4
+    length = tokens // stretches
+    parts = [jnp.zeros((states, channels), F32)] * stretches
+    for offset in range(length):
+        for index in range(stretches):
+            t = index * length + offset
+            decay = jnp.exp2(decay_step[t : t + 1, :] * rate)
+            parts[index] = decay * parts[index] + drive_step[t : t + 1, :] * in_map[:, t : t + 1]
+    state = parts[0]
+    for index in range(1, stretches):
+        spent = jnp.sum(step[index * length : (index + 1) * length], axis=0, keepdims=True)
+        state = jnp.exp2(spent * rate) * state + parts[index]
     message = join(state, last, send_ref.shape[2])
     for peer in range(send_ref.shape[0]):
         send_ref[peer] = message
@@ -320,8 +340,8 @@
     sums = jnp.zeros((16, tokens), F32)
     for peer in range(count):
         wide[peer * features : (peer + 1) * features, :] = in_ref[peer, 0:features, :]
-        sums = sums + in_ref[peer, features + 16 : features + 32, :].astype(F32)
-    scale = lax.rsqrt((sums[0:1] + sums[1:2]) / (count * features) + EPSILON)
+        sums = sums + in_ref[peer, features : features + 16, :].astype(F32)
+    scale = lax.rsqrt(square_sums(sums, features)[0] / (count * features) + EPSILON)
     in_map = maps_ref[0:states, :]
     out_map = maps_ref[states:, :]
     step = decay_step[...]
@@ -426,7 +446,7 @@
     arrived = lax.all_to_all(pieces, ("z", "x"), 0, 0, tiled=True)
     payload = call(
         place_body,
-        shape((features + 32, row_count), BF16),
+        shape((features + 16, row_count), BF16),
         [VMEM, VMEM],
         (arrived, my_gain),
     )

time: 87.9 us -> 87.8 us (level)
  no operation moved by 1% of the time
where the time goes in v8:
time: 87.8 us; the launch traced here: 86.5 us
  blocking collectives  45.3 us (52%)
  starting transfers between devices  17.1 us (19%)
  Pallas kernels  12.2 us (14%)
  waiting for transfers between devices  11.1 us (13%)
    all_gather x1, blocking collectives, local(): gathered = lax.all_gather(payload, 'chan', axis=0)  21.5 us
    all_gather x1, blocking collectives, local(): lows = lax.all_gather(low, 'chan', axis=0)  17.1 us
    all_to_all x1, starting transfers between devices, local(): arrived = lax.all_to_all(pieces, ('z', 'x'), 0, 0, tiled=True)  13.7 us
    pallas_call x8, Pallas kernels, call(): pl.pallas_call(body, out_shape=outs, in_specs=specs, out_specs=jax.tree.m...  12.2 us
    all_to_all x1, waiting for transfers between devices, local(): arrived = lax.all_to_all(pieces, ('z', 'x'), 0, 0, tiled=True)  6.98 us
    all_to_all x1, blocking collectives, local(): in_row_ends = lax.all_to_all(send, 'x', 0, 0, tiled=True)  6.74 us
    all_to_all x1, waiting for transfers between devices, local(): ends = lax.all_to_all(send, 'z', 0, 0, tiled=True)  4.1 us
    all_to_all x1, starting transfers between devices, local(): ends = lax.all_to_all(send, 'z', 0, 0, tiled=True)  3.36 us
  transfers between devices with their start and end apart: 2, of which 2 were waited for; matrix products, arithmetic and copies ran while one was open for 1% of the time, Pallas kernels for 6%

profile of v8, /device:TPU:1, one launch (start us, length us, event | category | flops | bytes accessed | tf_op | source)
XLA Modules:
  0.0 86.5 jit_solution(7400473887417408674)
XLA Ops:
  0.0 2.0 %shard_map.118 = (bf16[32,16,128]{2,1,0:T(8,128)(2,1)}, s32[1,128]{1,0:T(1,128)S(1)}) custom-call(s32[1]{0:T(128)} %bitcast.2.me, s32[16]{0:T(128)} %target_hbm.1, bf16[160,128]{1,0:T(8,128)(2,1)} %bitcast.19, s32[1,128]{1,0:T(1,128)} %bitcast.21), custom_call_target="tpu_custom_call" | custom-call | tf_op jit(solution)/shard_map/pallas_call | solution.py:39
  2.0 13.7 %all-to-all-start = ((bf16[32,16,128]{2,1,0:T(8,128)(2,1)}), bf16[32,16,128]{2,1,0:T(8,128)(2,1)S(1)}, u32[]{:S(2)}, u32[]{:S(2)}) async-start(bf16[32,16,128]{2,1,0:T(8,128)(2,1)} %get-tuple-element.25), calls=%async_computation | async-start | bytes 262144 | tf_op jit(solution)/shard_map/all_to_all | solution.py:446
  15.7 0.8 dynamic_slice.3
  16.5 1.6 %shard_map.120 = (bf16[320,2560]{1,0:T(8,128)(2,1)S(1)}, bf16[192,320]{1,0:T(8,128)(2,1)S(1)}, bf16[160,320]{1,0:T(8,128)(2,1)S(1)}, f32[16,320]{1,0:T(8,128)S(1...) custom-call(bf16[640,2560]{1,0:T(8,128)(2,1)} %bitcast.16, bf16[192,320]{1,0:T(8,128)(2,1)} %bitcast.18, ...), custom_call_target="tpu_custom_call" | custom-call | tf_op jit(solution)/shard_map/pallas_call | solution.py:39
  18.1 7.0 %all-to-all-done.in_ref = bf16[32,16,128]{2,1,0:T(8,128)(2,1)S(1)} async-done(((bf16[32,16,128]{2,1,0:T(8,128)(2,1)}), bf16[32,16,128]{2,1,0:T(8,128)(2,1)S(1)}, u32[]{:S(2)}, u32[]{:S(2)}) %all-to-all-start) | async-done | bytes 131104 | tf_op jit(solution)/shard_map/all_to_all | solution.py:446
  25.1 0.1 broadcast_in_dim.2.gain_ref
  25.2 0.8 shard_map.119
  25.9 21.5 %all-gather = bf16[2816,128]{1,0:T(8,128)(2,1)S(1)} all-gather(bf16[176,128]{1,0:T(8,128)(2,1)S(1)} %shard_map.119), channel_id=2, replica_groups=mesh['z'=8,'x'=4,'chan'=16] {'chan'}, dimensions={0}, use_global_device_ids=true | all-gather | bytes 765952 | tf_op jit(solution)/shard_map/all_gather | solution.py:453
  47.4 1.0 %shard_map.121 = (bf16[192,128]{1,0:T(8,128)(2,1)S(1)}, bf16[320,128]{1,0:T(8,128)(2,1)S(1)}) custom-call(bf16[16,176,128]{2,1,0:T(8,128)(2,1)S(1)} %bitcast.13, bf16[320,2560]{1,0:T(8,128)(2,1)S(1)} %get-tuple-element.27.weight_ref, f32[320,8]{1,0:T(8,128)S(1)} %get-tuple-element.28.taps_ref, bf16[192,320]{1,0:T(8,128)(2,1)S(1)} %get-tuple-element.29.proj_ref, ...), custom_call_target="tpu_custom_call" | custom-call | tf_op jit(solution)/shard_map/pallas_call | solution.py:39
  48.4 17.1 %all-gather.1 = bf16[3072,128]{1,0:T(8,128)(2,1)S(1)} all-gather(bf16[192,128]{1,0:T(8,128)(2,1)S(1)} %get-tuple-element.30), channel_id=3, replica_groups=mesh['z'=8,'x'=4,'chan'=16] {'chan'}, dimensions={0}, use_global_device_ids=true | all-gather | bytes 835584 | tf_op jit(solution)/shard_map/all_gather | solution.py:461
  65.5 1.2 %shard_map.122 = (bf16[4,16,384]{2,1,0:T(8,128)(2,1)S(1)}, f32[128,320]{1,0:T(8,128)S(1)}, f32[128,320]{1,0:T(8,128)S(1)}, f32[32,128]{1,0:T(8,128)S(1)}) custom-call(bf16[16,192,128]{2,1,0:T(8,128)(2,1)S(1)} %bitcast.15, bf16[320,128]{1,0:T(8,128)(2,1)S(1)} %get-tuple-element.31.act_ref, bf16[160,320]{1,0:T(8,128)(2,1)S(1)} %get-tuple-element.32.dtw_ref, ...), custom_call_target="tpu_custom_call" | custom-call | tf_op jit(solution)/shard_map/pallas_call | solution.py:39
  66.7 6.7 %all_to_all.15.in_ref = bf16[4,16,384]{2,1,0:T(8,128)(2,1)S(1)} all-to-all(bf16[4,16,384]{2,1,0:T(8,128)(2,1)S(1)} %get-tuple-element.36), channel_id=1, replica_groups=mesh['z'=8,'x'=4,'chan'=16] {'x'}, dimensions={0} | all-to-all | bytes 98304 | tf_op jit(solution)/shard_map/all_to_all | solution.py:475
  73.5 1.1 %shard_map.123 = (bf16[8,16,384]{2,1,0:T(8,128)(2,1)}, f32[16,320]{1,0:T(8,128)S(1)}, f32[8,320]{1,0:T(8,128)S(1)}) custom-call(s32[1]{0:T(128)} %bitcast.1.me, bf16[4,16,384]{2,1,0:T(8,128)(2,1)S(1)} %all_to_all.15.in_ref, f32[16,320]{1,0:T(8,128)S(1)} %get-tuple-element.33.rate_ref), custom_call_target="tpu_custom_call" | custom-call | tf_op jit(solution)/shard_map/pallas_call | solution.py:39
  74.5 3.4 %all-to-all-start.2 = ((bf16[8,16,384]{2,1,0:T(8,128)(2,1)}), bf16[8,16,384]{2,1,0:T(8,128)(2,1)S(1)}, u32[]{:S(2)}, u32[]{:S(2)}) async-start(bf16[8,16,384]{2,1,0:T(8,128)(2,1)} %get-tuple-element.37), calls=%async_computation.2 | async-start | bytes 196608 | tf_op jit(solution)/shard_map/all_to_all | solution.py:499
  77.9 3.4 %shard_map.124 = (f32[128,320]{1,0:T(8,128)S(1)}, bf16[16,128,320]{2,1,0:T(8,128)(2,1)S(1)}) custom-call(bf16[16,176,128]{2,1,0:T(8,128)(2,1)S(1)} %bitcast.14, bf16[640,2560]{1,0:T(8,128)(2,1)} %bitcast.17, bf16[320,128]{1,0:T(8,128)(2,1)S(1)} %get-tuple-element.31.act_ref, f32[16,320]{1,0:T(8,128)S(1)} %get-tuple-element.33.rate_ref, ...), custom_call_target="tpu_custom_call" | custom-call | tf_op jit(solution)/shard_map/pallas_call | solution.py:39
  81.3 4.1 %all-to-all-done.2.in_ref = bf16[8,16,384]{2,1,0:T(8,128)(2,1)S(1)} async-done(((bf16[8,16,384]{2,1,0:T(8,128)(2,1)}), bf16[8,16,384]{2,1,0:T(8,128)(2,1)S(1)}, u32[]{:S(2)}, u32[]{:S(2)}) %all-to-all-start.2) | async-done | bytes 98336 | tf_op jit(solution)/shard_map/all_to_all | solution.py:499
  85.4 1.2 %shard_map.125 = bf16[320,128]{1,0:T(8,128)(2,1)} custom-call(s32[1]{0:T(128)} %bitcast.me, bf16[8,16,384]{2,1,0:T(8,128)(2,1)S(1)} %all-to-all-done.2.in_ref, f32[16,320]{1,0:T(8,128)S(1)} %get-tuple-element.33.rate_ref, f32[16,320]{1,0:T(8,128)S(1)} %get-tuple-element.38.before_ref, f32[8,320]{1,0:T(8,128)S(1)} %get-tuple-element.39.row_ref.length_ref, ...), custom_call_target="tpu_custom_call" | custom-call | tf_op jit(solution)/shard_map/pallas_call | solution.py:39
Async XLA Ops:
  2.0 23.1 %all-to-all-start = ((bf16[32,16,128]{2,1,0:T(8,128)(2,1)}), bf16[32,16,128]{2,1,0:T(8,128)(2,1)S(1)}, u32[]{:S(2)}, u32[]{:S(2)}) async-start(bf16[32,16,128]{2,1,0:T(8,128)(2,1)} %get-tuple-element.25), calls=%async_computation | async-start | bytes 262144 | tf_op jit(solution)/shard_map/all_to_all | solution.py:446
  74.5 10.9 %all-to-all-start.2 = ((bf16[8,16,384]{2,1,0:T(8,128)(2,1)}), bf16[8,16,384]{2,1,0:T(8,128)(2,1)S(1)}, u32[]{:S(2)}, u32[]{:S(2)}) async-start(bf16[8,16,384]{2,1,0:T(8,128)(2,1)} %get-tuple-element.37), calls=%async_computation.2 | async-start | bytes 196608 | tf_op jit(solution)/shard_map/all_to_all | solution.py:499

commit v9 on v8

--- a/solution.py
+++ b/solution.py
@@ -387,7 +387,7 @@
     scanned = out_in_ref[...]
     for index in range(states):
         scanned = scanned + share_ref[index].astype(F32) * state[index : index + 1, :]
-    mixed_ref[...] = jnp.transpose(scanned).astype(BF16)
+    mixed_ref[...] = jnp.transpose(scanned.astype(BF16))
 
 
 def local(

time: 87.8 us -> 87.8 us (level)
  no operation moved by 1% of the time
where the time goes in v9:
time: 87.8 us; the launch traced here: 86.5 us
  blocking collectives  45.3 us (52%)
  starting transfers between devices  17.1 us (19%)
  Pallas kernels  12.1 us (14%)
  waiting for transfers between devices  11.1 us (13%)
    all_gather x1, blocking collectives, local(): gathered = lax.all_gather(payload, 'chan', axis=0)  21.5 us
    all_gather x1, blocking collectives, local(): lows = lax.all_gather(low, 'chan', axis=0)  17.1 us
    all_to_all x1, starting transfers between devices, local(): arrived = lax.all_to_all(pieces, ('z', 'x'), 0, 0, tiled=True)  13.7 us
    pallas_call x8, Pallas kernels, call(): pl.pallas_call(body, out_shape=outs, in_specs=specs, out_specs=jax.tree.m...  12.1 us
    all_to_all x1, waiting for transfers between devices, local(): arrived = lax.all_to_all(pieces, ('z', 'x'), 0, 0, tiled=True)  6.98 us
    all_to_all x1, blocking collectives, local(): in_row_ends = lax.all_to_all(send, 'x', 0, 0, tiled=True)  6.74 us
    all_to_all x1, waiting for transfers between devices, local(): ends = lax.all_to_all(send, 'z', 0, 0, tiled=True)  4.1 us
    all_to_all x1, starting transfers between devices, local(): ends = lax.all_to_all(send, 'z', 0, 0, tiled=True)  3.36 us
  transfers between devices with their start and end apart: 2, of which 2 were waited for; matrix products, arithmetic and copies ran while one was open for 1% of the time, Pallas kernels for 6%

profile of v9, /device:TPU:1, one launch (start us, length us, event | category | flops | bytes accessed | tf_op | source)
XLA Modules:
  0.0 86.5 jit_solution(478360536931349863)
XLA Ops:
  0.0 2.0 %shard_map.118 = (bf16[32,16,128]{2,1,0:T(8,128)(2,1)}, s32[1,128]{1,0:T(1,128)S(1)}) custom-call(s32[1]{0:T(128)} %bitcast.2.me, s32[16]{0:T(128)} %target_hbm.1, bf16[160,128]{1,0:T(8,128)(2,1)} %bitcast.19, s32[1,128]{1,0:T(1,128)} %bitcast.21), custom_call_target="tpu_custom_call" | custom-call | tf_op jit(solution)/shard_map/pallas_call | solution.py:39
  2.0 13.7 %all-to-all-start = ((bf16[32,16,128]{2,1,0:T(8,128)(2,1)}), bf16[32,16,128]{2,1,0:T(8,128)(2,1)S(1)}, u32[]{:S(2)}, u32[]{:S(2)}) async-start(bf16[32,16,128]{2,1,0:T(8,128)(2,1)} %get-tuple-element.25), calls=%async_computation | async-start | bytes 262144 | tf_op jit(solution)/shard_map/all_to_all | solution.py:446
  15.7 0.8 dynamic_slice.3
  16.5 1.6 %shard_map.120 = (bf16[320,2560]{1,0:T(8,128)(2,1)S(1)}, bf16[192,320]{1,0:T(8,128)(2,1)S(1)}, bf16[160,320]{1,0:T(8,128)(2,1)S(1)}, f32[16,320]{1,0:T(8,128)S(1...) custom-call(bf16[640,2560]{1,0:T(8,128)(2,1)} %bitcast.16, bf16[192,320]{1,0:T(8,128)(2,1)} %bitcast.18, ...), custom_call_target="tpu_custom_call" | custom-call | tf_op jit(solution)/shard_map/pallas_call | solution.py:39
  18.1 7.0 %all-to-all-done.in_ref = bf16[32,16,128]{2,1,0:T(8,128)(2,1)S(1)} async-done(((bf16[32,16,128]{2,1,0:T(8,128)(2,1)}), bf16[32,16,128]{2,1,0:T(8,128)(2,1)S(1)}, u32[]{:S(2)}, u32[]{:S(2)}) %all-to-all-start) | async-done | bytes 131104 | tf_op jit(solution)/shard_map/all_to_all | solution.py:446
  25.1 0.1 broadcast_in_dim.2.gain_ref
  25.2 0.8 shard_map.119
  25.9 21.5 %all-gather = bf16[2816,128]{1,0:T(8,128)(2,1)S(1)} all-gather(bf16[176,128]{1,0:T(8,128)(2,1)S(1)} %shard_map.119), channel_id=2, replica_groups=mesh['z'=8,'x'=4,'chan'=16] {'chan'}, dimensions={0}, use_global_device_ids=true | all-gather | bytes 765952 | tf_op jit(solution)/shard_map/all_gather | solution.py:453
  47.4 1.0 %shard_map.121 = (bf16[192,128]{1,0:T(8,128)(2,1)S(1)}, bf16[320,128]{1,0:T(8,128)(2,1)S(1)}) custom-call(bf16[16,176,128]{2,1,0:T(8,128)(2,1)S(1)} %bitcast.13, bf16[320,2560]{1,0:T(8,128)(2,1)S(1)} %get-tuple-element.27.weight_ref, f32[320,8]{1,0:T(8,128)S(1)} %get-tuple-element.28.taps_ref, bf16[192,320]{1,0:T(8,128)(2,1)S(1)} %get-tuple-element.29.proj_ref, ...), custom_call_target="tpu_custom_call" | custom-call | tf_op jit(solution)/shard_map/pallas_call | solution.py:39
  48.4 17.1 %all-gather.1 = bf16[3072,128]{1,0:T(8,128)(2,1)S(1)} all-gather(bf16[192,128]{1,0:T(8,128)(2,1)S(1)} %get-tuple-element.30), channel_id=3, replica_groups=mesh['z'=8,'x'=4,'chan'=16] {'chan'}, dimensions={0}, use_global_device_ids=true | all-gather | bytes 835584 | tf_op jit(solution)/shard_map/all_gather | solution.py:461
  65.5 1.2 %shard_map.122 = (bf16[4,16,384]{2,1,0:T(8,128)(2,1)S(1)}, f32[128,320]{1,0:T(8,128)S(1)}, f32[128,320]{1,0:T(8,128)S(1)}, f32[32,128]{1,0:T(8,128)S(1)}) custom-call(bf16[16,192,128]{2,1,0:T(8,128)(2,1)S(1)} %bitcast.15, bf16[320,128]{1,0:T(8,128)(2,1)S(1)} %get-tuple-element.31.act_ref, bf16[160,320]{1,0:T(8,128)(2,1)S(1)} %get-tuple-element.32.dtw_ref, ...), custom_call_target="tpu_custom_call" | custom-call | tf_op jit(solution)/shard_map/pallas_call | solution.py:39
  66.7 6.7 %all_to_all.15.in_ref = bf16[4,16,384]{2,1,0:T(8,128)(2,1)S(1)} all-to-all(bf16[4,16,384]{2,1,0:T(8,128)(2,1)S(1)} %get-tuple-element.36), channel_id=1, replica_groups=mesh['z'=8,'x'=4,'chan'=16] {'x'}, dimensions={0} | all-to-all | bytes 98304 | tf_op jit(solution)/shard_map/all_to_all | solution.py:475
  73.5 1.1 %shard_map.123 = (bf16[8,16,384]{2,1,0:T(8,128)(2,1)}, f32[16,320]{1,0:T(8,128)S(1)}, f32[8,320]{1,0:T(8,128)S(1)}) custom-call(s32[1]{0:T(128)} %bitcast.1.me, bf16[4,16,384]{2,1,0:T(8,128)(2,1)S(1)} %all_to_all.15.in_ref, f32[16,320]{1,0:T(8,128)S(1)} %get-tuple-element.33.rate_ref), custom_call_target="tpu_custom_call" | custom-call | tf_op jit(solution)/shard_map/pallas_call | solution.py:39
  74.5 3.4 %all-to-all-start.2 = ((bf16[8,16,384]{2,1,0:T(8,128)(2,1)}), bf16[8,16,384]{2,1,0:T(8,128)(2,1)S(1)}, u32[]{:S(2)}, u32[]{:S(2)}) async-start(bf16[8,16,384]{2,1,0:T(8,128)(2,1)} %get-tuple-element.37), calls=%async_computation.2 | async-start | bytes 196608 | tf_op jit(solution)/shard_map/all_to_all | solution.py:499
  77.9 3.4 %shard_map.124 = (f32[128,320]{1,0:T(8,128)S(1)}, bf16[16,128,320]{2,1,0:T(8,128)(2,1)S(1)}) custom-call(bf16[16,176,128]{2,1,0:T(8,128)(2,1)S(1)} %bitcast.14, bf16[640,2560]{1,0:T(8,128)(2,1)} %bitcast.17, bf16[320,128]{1,0:T(8,128)(2,1)S(1)} %get-tuple-element.31.act_ref, f32[16,320]{1,0:T(8,128)S(1)} %get-tuple-element.33.rate_ref, ...), custom_call_target="tpu_custom_call" | custom-call | tf_op jit(solution)/shard_map/pallas_call | solution.py:39
  81.3 4.1 %all-to-all-done.2.in_ref = bf16[8,16,384]{2,1,0:T(8,128)(2,1)S(1)} async-done(((bf16[8,16,384]{2,1,0:T(8,128)(2,1)}), bf16[8,16,384]{2,1,0:T(8,128)(2,1)S(1)}, u32[]{:S(2)}, u32[]{:S(2)}) %all-to-all-start.2) | async-done | bytes 98336 | tf_op jit(solution)/shard_map/all_to_all | solution.py:499
  85.4 1.1 %shard_map.125 = bf16[320,128]{1,0:T(8,128)(2,1)} custom-call(s32[1]{0:T(128)} %bitcast.me, bf16[8,16,384]{2,1,0:T(8,128)(2,1)S(1)} %all-to-all-done.2.in_ref, f32[16,320]{1,0:T(8,128)S(1)} %get-tuple-element.33.rate_ref, f32[16,320]{1,0:T(8,128)S(1)} %get-tuple-element.38.before_ref, f32[8,320]{1,0:T(8,128)S(1)} %get-tuple-element.39.row_ref.length_ref, ...), custom_call_target="tpu_custom_call" | custom-call | tf_op jit(solution)/shard_map/pallas_call | solution.py:39
Async XLA Ops:
  2.0 23.1 %all-to-all-start = ((bf16[32,16,128]{2,1,0:T(8,128)(2,1)}), bf16[32,16,128]{2,1,0:T(8,128)(2,1)S(1)}, u32[]{:S(2)}, u32[]{:S(2)}) async-start(bf16[32,16,128]{2,1,0:T(8,128)(2,1)} %get-tuple-element.25), calls=%async_computation | async-start | bytes 262144 | tf_op jit(solution)/shard_map/all_to_all | solution.py:446
  74.5 10.9 %all-to-all-start.2 = ((bf16[8,16,384]{2,1,0:T(8,128)(2,1)}), bf16[8,16,384]{2,1,0:T(8,128)(2,1)S(1)}, u32[]{:S(2)}, u32[]{:S(2)}) async-start(bf16[8,16,384]{2,1,0:T(8,128)(2,1)} %get-tuple-element.37), calls=%async_computation.2 | async-start | bytes 196608 | tf_op jit(solution)/shard_map/all_to_all | solution.py:499
